TPU v7x, 32 devices: a whole 2x2x4 slice. The times are simulated.
32 devices in a mesh: dp: 8 (over y, x, core), mp: 4 (over z).
Axes of the slice: x: 2, y: 2, z: 4, core: 2. Of those that a mesh axis runs over, the one named last changes fastest.
Arguments:
- grid_latent: bfloat16 [8, 1024, 1024], P('dp', 'mp'), may hold values from -6 to 6
- mesh_latent: bfloat16 [8, 512, 1024], P('dp', 'mp'), may hold values from -6 to 6
- edge_source: int32 [8, 3072], P('dp', 'mp'), may hold values from 0 to 1023, as said below
- edge_dest: int32 [8, 3072], P('dp', 'mp'), may hold values from 0 to 511, as said below
- edge_count: int32 [8, 4], P('dp', 'mp'), may hold values from 256 to 768, as said below
- edge_attr: float32 [8, 4, 3072], P('dp', None, 'mp'), may hold values from -5 to 5
- w_attr: float32 [4, 1024], replicated, may hold values from -3 to 3
- w_in: bfloat16 [1024, 1024], replicated, may hold values from -0.1875 to 0.1875
- w_out: bfloat16 [1024, 1024], replicated, may hold values from -0.1875 to 0.1875
- w_qkv: bfloat16 [3, 1024, 1024], P(None, None, 'mp')
- w_o: bfloat16 [1024, 1024], P('mp'), may hold values from -0.1875 to 0.1875
- cotangent: bfloat16 [8, 512, 1024], P('dp', 'mp'), may hold values from -6 to 6
Outputs:
- d_grid: bfloat16 [8, 1024, 1024], P('dp', 'mp')
- d_mesh: bfloat16 [8, 512, 1024], P('dp', 'mp')
- d_w_attr: float32 [4, 1024], replicated
- d_w_in: float32 [1024, 1024], P('dp', 'mp')
- d_w_out: float32 [1024, 1024], P('dp', 'mp')
- d_w_qkv: float32 [3, 1024, 1024], P(None, 'dp', 'mp')
- d_w_o: float32 [1024, 1024], P('mp', 'dp')
Inputs may be any that keep to these rules, and one draw needn't show every extreme that they name: `edge_source`: edge slots of band b (positions b * 768 to (b + 1) * 768 - 1 of a sample) name grid points of band b, rows b * 256 to (b + 1) * 256 - 1. `edge_dest`: edge slots of band b name mesh nodes of band b - 1, b or b + 1 (bands of 128 nodes each). `edge_count`: the first and last bands of every sample are full.
All inputs are finite; a program needn't handle non-finite values.
Results may differ from a plain program's by a relative error of at most 0.025.
Values may be sent and summed in bfloat16 or wider, within the bound.
A program may use at most 128 MiB of HBM per device.

v0:
```python
import jax
import jax.numpy as jnp
from jax import lax
from jax.sharding import PartitionSpec as P

HDIM = 64


EPS = 1e-06


def shifted(block, axis, distance):
    devices = range(lax.axis_size(axis))
    route = [(i - distance, i) for i in devices if i - distance in devices]
    return lax.ppermute(block, axis, route)


def with_halo(block, sides, width):
    for axis, dim in sides:
        count = lax.axis_size(axis)
        forward = [(i, i + 1) for i in range(count - 1)]
        backward = [(target, source) for source, target in forward]
        low = lax.ppermute(
            lax.slice_in_dim(block, block.shape[dim] - width, None, axis=dim), axis, forward
        )
        high = lax.ppermute(lax.slice_in_dim(block, 0, width, axis=dim), axis, backward)
        block = jnp.concatenate([low, block, high], axis=dim)
    return block


def shards(
    grid_latent,
    mesh_latent,
    edge_source,
    edge_dest,
    edge_count,
    edge_attr,
    w_attr,
    w_in,
    w_out,
    w_qkv,
    w_o,
    cotangent,
):
    band = lax.axis_index("mp")
    grid_rows = grid_latent.shape[1]
    nodes = mesh_latent.shape[1]
    edges = edge_source.shape[1]
    grid = grid_latent[0]
    live = (jnp.arange(edges, dtype=jnp.int32) < edge_count[0, 0]).astype(jnp.float32)[:, None]
    source_local = edge_source[0] - band * grid_rows
    dest_local = edge_dest[0] - (band - 1) * nodes
    projected = jnp.dot(grid, w_in, preferred_element_type=jnp.float32)
    attr_terms = lax.dot_general(
        edge_attr[0],
        w_attr,
        (((0,), (0,)), ((), ())),
        precision=lax.Precision.HIGHEST,
        preferred_element_type=jnp.float32,
    )
    preact = projected[source_local] + attr_terms
    hidden = (jax.nn.silu(preact) * live).astype(jnp.bfloat16)
    message = jnp.dot(hidden, w_out, preferred_element_type=jnp.float32).astype(jnp.bfloat16)
    dest_table = (dest_local[:, None] == jnp.arange(3 * nodes, dtype=jnp.int32)[None, :]).astype(
        jnp.bfloat16
    )
    partial_rows = lax.dot_general(
        dest_table, message, (((0,), (0,)), ((), ())), preferred_element_type=jnp.float32
    )
    from_below = shifted(partial_rows[2 * nodes :], "mp", 1)
    from_above = shifted(partial_rows[:nodes], "mp", -1)
    node = (
        mesh_latent[0].astype(jnp.float32)
        + partial_rows[nodes : 2 * nodes]
        + from_below
        + from_above
    )
    inv = lax.rsqrt(jnp.mean(node * node, axis=-1, keepdims=True) + EPS)
    normed = (node * inv).astype(jnp.bfloat16)
    all_normed, all_cot = (
        lax.all_gather(normed, "mp", axis=0, tiled=True),
        lax.all_gather(cotangent[0], "mp", axis=0, tiled=True),
    )
    total = all_normed.shape[0]
    width = w_qkv.shape[2]
    local_heads = width // HDIM
    qkv = jnp.einsum("nc,icd->ind", all_normed, w_qkv, preferred_element_type=jnp.float32).astype(
        jnp.bfloat16
    )
    qkv = qkv.reshape(3, total, local_heads, HDIM)
    query, keys, values = (qkv[0], qkv[1], qkv[2])
    d_att = lax.dot_general(
        all_cot, w_o, (((1,), (1,)), ((), ())), preferred_element_type=jnp.float32
    ).astype(jnp.bfloat16)
    d_att = d_att.reshape(total, local_heads, HDIM)
    block = min(512, total)
    scale = HDIM ** (-0.5)

    def attend_block(carry, index):
        key_acc, value_acc = carry
        start = index * block
        query_blk = lax.dynamic_slice_in_dim(query, start, block, 0)
        grad_blk = lax.dynamic_slice_in_dim(d_att, start, block, 0)
        scores = (
            jnp.einsum("qhd,khd->hqk", query_blk, keys, preferred_element_type=jnp.float32) * scale
        )
        probs = jax.nn.softmax(scores, axis=-1)
        probs_b = probs.astype(jnp.bfloat16)
        attended = jnp.einsum(
            "hqk,khd->qhd", probs_b, values, preferred_element_type=jnp.float32
        ).astype(jnp.bfloat16)
        dprob = jnp.einsum("qhd,khd->hqk", grad_blk, values, preferred_element_type=jnp.float32)
        delta = jnp.sum(probs * dprob, axis=-1, keepdims=True)
        dscore = (probs * (dprob - delta) * scale).astype(jnp.bfloat16)
        dquery = jnp.einsum(
            "hqk,khd->qhd", dscore, keys, preferred_element_type=jnp.float32
        ).astype(jnp.bfloat16)
        key_acc = key_acc + jnp.einsum(
            "hqk,qhd->khd", dscore, query_blk, preferred_element_type=jnp.float32
        )
        value_acc = value_acc + jnp.einsum(
            "hqk,qhd->khd", probs_b, grad_blk, preferred_element_type=jnp.float32
        )
        return ((key_acc, value_acc), (attended, dquery))

    empty = jnp.zeros((total, local_heads, HDIM), jnp.float32)
    sums, blocks = lax.scan(
        attend_block, (empty, empty), jnp.arange(total // block, dtype=jnp.int32)
    )
    attended = blocks[0].reshape(total, width)
    dquery = blocks[1].reshape(total, width)
    dkeys = sums[0].astype(jnp.bfloat16).reshape(total, width)
    dvalues = sums[1].astype(jnp.bfloat16).reshape(total, width)
    dqkv = jnp.stack([dquery, dkeys, dvalues])
    dw_o = lax.dot_general(
        attended, all_cot, (((0,), (0,)), ((), ())), preferred_element_type=jnp.float32
    )
    dw_qkv = jnp.einsum("nc,ind->icd", all_normed, dqkv, preferred_element_type=jnp.float32)
    sum_qkv, sum_o = (
        lax.psum_scatter(dw_qkv.astype(jnp.bfloat16), "dp", scatter_dimension=1, tiled=True).astype(
            jnp.float32
        ),
        lax.psum_scatter(dw_o.astype(jnp.bfloat16), "dp", scatter_dimension=1, tiled=True).astype(
            jnp.float32
        ),
    )
    dx = lax.psum_scatter(
        jnp.einsum("ind,icd->nc", dqkv, w_qkv, preferred_element_type=jnp.float32).astype(
            jnp.bfloat16
        ),
        "mp",
        scatter_dimension=0,
        tiled=True,
    ).astype(jnp.float32)
    dnode = (
        cotangent[0].astype(jnp.float32)
        + inv * dx
        - node * inv * inv * inv * jnp.mean(dx * node, axis=-1, keepdims=True)
    )
    d_mesh = dnode.astype(jnp.bfloat16)
    beside_all = with_halo(d_mesh, (("mp", 0),), nodes)
    dmessage = (beside_all[dest_local].astype(jnp.float32) * live).astype(jnp.bfloat16)
    dw_out = lax.dot_general(
        hidden, dmessage, (((0,), (0,)), ((), ())), preferred_element_type=jnp.float32
    )
    dhidden = lax.dot_general(
        dmessage, w_out, (((1,), (1,)), ((), ())), preferred_element_type=jnp.float32
    )
    sigma = jax.nn.sigmoid(preact)
    dpre = dhidden * sigma * (1.0 + preact * (1.0 - sigma)) * live
    dw_attr = jnp.dot(
        edge_attr[0], dpre, precision=lax.Precision.HIGHEST, preferred_element_type=jnp.float32
    )
    source_table = (
        source_local[:, None] == jnp.arange(grid_rows, dtype=jnp.int32)[None, :]
    ).astype(jnp.bfloat16)
    dproj = lax.dot_general(
        source_table,
        dpre.astype(jnp.bfloat16),
        (((0,), (0,)), ((), ())),
        preferred_element_type=jnp.float32,
    ).astype(jnp.bfloat16)
    dw_in = lax.dot_general(
        grid, dproj, (((0,), (0,)), ((), ())), preferred_element_type=jnp.float32
    )
    d_grid = lax.dot_general(
        dproj, w_in, (((1,), (1,)), ((), ())), preferred_element_type=jnp.float32
    ).astype(jnp.bfloat16)
    sum_attr = lax.psum(dw_attr, ("dp", "mp"))
    first_in, first_out = (
        lax.psum_scatter(dw_in.astype(jnp.bfloat16), "dp", scatter_dimension=0, tiled=True).astype(
            jnp.float32
        ),
        lax.psum_scatter(dw_out.astype(jnp.bfloat16), "dp", scatter_dimension=0, tiled=True).astype(
            jnp.float32
        ),
    )
    sum_in, sum_out = (
        lax.psum_scatter(
            first_in.astype(jnp.bfloat16), "mp", scatter_dimension=1, tiled=True
        ).astype(jnp.float32),
        lax.psum_scatter(
            first_out.astype(jnp.bfloat16), "mp", scatter_dimension=1, tiled=True
        ).astype(jnp.float32),
    )
    return (d_grid[None], d_mesh[None], sum_attr, sum_in, sum_out, sum_qkv, sum_o)


def solution(mesh):
    return jax.shard_map(
        shards,
        mesh=mesh,
        in_specs=(
            P("dp", "mp", None),
            P("dp", "mp", None),
            P("dp", "mp"),
            P("dp", "mp"),
            P("dp", "mp"),
            P("dp", None, "mp"),
            P(),
            P(),
            P(),
            P(None, None, "mp"),
            P("mp", None),
            P("dp", "mp", None),
        ),
        out_specs=(
            P("dp", "mp", None),
            P("dp", "mp", None),
            P(),
            P("dp", "mp"),
            P("dp", "mp"),
            P(None, "dp", "mp"),
            P("mp", "dp"),
        ),
        check_vma=False,
    )
```

profile of v0, /device:TPU:0, one launch (start us, length us, event | category | flops | bytes accessed | tf_op | source)
XLA Modules:
  0.0 393.5 jit_solution(13935290074789890285)
XLA Ops:
  11.9 3.7 gather_fusion
  15.6 5.6 %convolution_add_fusion = f32[768,1024]{1,0:T(8,128)} fusion(f32[768,1024]{1,0:T(8,128)} %gather_fusion, f32[4,1024]{1,0:T(4,128)S(1)} %copy-done.11, f32[1,4,768]{2,1,0:T(4,128)S(1)} %copy-done.10), kind=kOutput, calls=%fused_computation.22 | convolution fusion | flops 38535168 | bytes 6320128 | tf_op jit(solution)/shard_map/dot_general | solution.py:54
  21.2 5.6 %fusion.31 = f32[384,1024]{1,0:T(8,128)} fusion(bf16[1024,1024]{1,0:T(8,128)(2,1)S(1)} %copy-done, s32[768]{0:T(1024)S(1)} %subtract_reduce_fusion, f32[768,1024]{1,0:T(8,128)} %convolution_add_fusion, f32[768]{0:T(1024)S(1)} %fusion.53), kind=kOutput, calls=%fused_computation.41 | convolution fusion | flops 2220392448 | bytes 6821888 | tf_op jit(solution)/shard_map/dot_general | solution.py:67
  28.1 5.0 %collective-permute-start = (f32[128,1024]{1,0:T(8,128)S(1)}, f32[128,1024]{1,0:T(8,128)S(1)}, u32[]{:S(2)}, u32[]{:S(2)}) collective-permute-start(f32[128,1024]{1,0:T(8,128)S(1)} %get-tuple-element.57), channel_id=1, source_target_pairs={{0,1},{1,2},{2,3},{4,5},{5,6},{6,7},{8,9},{9,10},{10,11},{12,13},{... | collective-permute-start | bytes 1572872 | tf_op jit(solution)/shard_map/ppermute | solution.py:15
  34.3 14.6 %collective-permute-done = f32[128,1024]{1,0:T(8,128)S(1)} collective-permute-done((f32[128,1024]{1,0:T(8,128)S(1)}, f32[128,1024]{1,0:T(8,128)S(1)}, u32[]{:S(2)}, u32[]{:S(2)}) %collective-permute-start) | collective-permute-done | bytes 524320 | tf_op jit(solution)/shard_map/ppermute | solution.py:15
  48.9 2.5 collective-permute-done.1
  55.6 25.6 %all-gather.4.cloned.1.call-done = bf16[512,1024]{1,0:T(8,128)(2,1)} async-done(((bf16[128,1024]{1,0:T(8,128)(2,1)}), bf16[512,1024]{1,0:T(8,128)(2,1)}) %all-gather.4.cloned.1.call-update) | async-done | bytes 1048592 | tf_op jit(solution)/shard_map/all_gather | solution.py:81
  81.3 2.8 fusion.20
  84.8 4.4 %fusion.66 = (f32[4,512]{1,0:T(4,128)S(1)}, f32[4,512,512]{1,2,0:T(8,128)}) fusion(bf16[512,4,64]{0,2,1:T(8,128)(2,1)S(1)} %bitcast.105, bf16[512,4,64]{0,2,1:T(8,128)(2,1)} %bitcast.107), kind=kOutput, calls=%fused_computation.92 | convolution fusion | flops 137363968 | bytes 4726784 | tf_op jit(solution)/shard_map/while/body/eval_jaxpr/sub | solution.py:107
  89.2 2.7 fusion.67
  91.9 8.4 %fusion.25 = bf16[4,64,512]{2,1,0:T(8,128)(2,1)} fusion(bf16[512,4,64]{0,2,1:T(8,128)(2,1)} %bitcast.108, f32[4,512,512]{1,2,0:T(8,128)} %fusion.67, f32[4,512,512]{1,2,0:T(8,128)} %get-tuple-element.63, f32[4,512]{1,0:T(4,128)S(1)} %get-tuple-element.62), kind=kOutput, calls=%fused_computation.35 | convolution fusion | flops 141691392 | bytes 8921088 | tf_op jit(solution)/shard_map/while/body/eval_jaxpr/hqk,khd->qhd/dot_general | solution.py:115
  100.3 8.1 %fusion.28 = bf16[4,64,512]{2,1,0:T(8,128)(2,1)} fusion(bf16[512,4,64]{0,2,1:T(8,128)(2,1)S(1)} %bitcast.106, f32[4,512,512]{1,2,0:T(8,128)} %fusion.67, f32[4,512,512]{1,2,0:T(8,128)} %get-tuple-element.63, f32[4,512]{1,0:T(4,128)S(1)} %get-tuple-element.62), kind=kOutput, calls=%fused_computation.36 | convolution fusion | flops 141691392 | bytes 8921088 | tf_op jit(solution)/shard_map/while/body/eval_jaxpr/hqk,qhd->khd/dot_general | solution.py:118
  108.4 3.7 convolution_convert_fusion.7
  116.8 3.6 bitcast_convert_fusion
  120.5 26.7 %reduce-scatter.14.cloned.1.call-done = bf16[128,1024]{1,0:T(8,128)(2,1)} async-done(((bf16[512,1024]{1,0:T(8,128)(2,1)}), bf16[128,1024]{1,0:T(8,128)(2,1)}) %reduce-scatter.14.cloned.1.call-update) | async-done | bytes 262160 | tf_op jit(solution)/shard_map/reduce_scatter | solution.py:147
  152.2 4.3 %collective-permute-done.2 = bf16[128,1024]{1,0:T(8,128)(2,1)S(1)} collective-permute-done((bf16[128,1024]{1,0:T(8,128)(2,1)S(1)}, bf16[128,1024]{1,0:T(8,128)(2,1)S(1)}, u32[]{:S(2)}, u32[]{:S(2)}) %collective-permute-start.2) | collective-permute-done | bytes 262176 | tf_op jit(solution)/shard_map/ppermute | solution.py:23
  156.5 4.5 %collective-permute-done.3 = bf16[128,1024]{1,0:T(8,128)(2,1)S(1)} collective-permute-done((bf16[128,1024]{1,0:T(8,128)(2,1)S(1)}, bf16[128,1024]{1,0:T(8,128)(2,1)S(1)}, u32[]{:S(2)}, u32[]{:S(2)}) %collective-permute-start.3) | collective-permute-done | bytes 262176 | tf_op jit(solution)/shard_map/ppermute | solution.py:26
  161.1 3.6 gather_fusion.1
  164.7 5.9 %convolution_convert_fusion = bf16[1024,1024]{1,0:T(8,128)(2,1)} fusion(bf16[768,1024]{1,0:T(8,128)(2,1)} %gather_fusion.1, f32[768]{0:T(1024)S(1)} %fusion.53, f32[768,1024]{1,0:T(8,128)} %convolution_add_fusion), kind=kOutput, calls=%fused_computation.23 | convolution fusion | flops 1618739200 | bytes 6818816 | tf_op jit(solution)/shard_map/dot_general | solution.py:163
  170.9 2.8 convolution_convert_fusion.6
  175.3 3.5 fusion.19
  178.8 4.2 %copy.60 = bf16[3,1024,256]{2,0,1:T(4,128)(2,1)} copy(bf16[3,1024,256]{1,2,0:T(8,128)(2,1)} %fusion.19) | data formatting | bytes 3145728
  183.0 3.2 copy.64
  186.2 4.9 %multiply_multiply_fusion = f32[768,1024]{1,0:T(8,128)S(1)} fusion(f32[768,1024]{1,0:T(8,128)} %convolution_add_fusion, bf16[1024,1024]{1,0:T(8,128)(2,1)S(1)} %copy-done, f32[768]{0:T(1024)S(1)} %fusion.53, bf16[768,1024]{1,0:T(8,128)(2,1)} %gather_fusion.1), kind=kOutput, calls=%fused_computation.10 | convolution fusion | flops 1620049920 | bytes 9964544 | tf_op jit(solution)/shard_map/dot_general | solution.py:166
  196.0 4.0 %copy.58 = bf16[1024,1024]{1,0:T(8,128)(2,1)} copy(bf16[1024,1024]{0,1:T(8,128)(2,1)} %convert_bitcast_fusion) | data formatting | bytes 4194304
  200.0 11.3 %reduce-scatter.18.cloned.1.call-done = bf16[128,1024]{1,0:T(8,128)(2,1)} async-done(((bf16[1024,1024]{1,0:T(8,128)(2,1)}), bf16[128,1024]{1,0:T(8,128)(2,1)}) %reduce-scatter.18.cloned.1.call-update) | async-done | bytes 262160 | tf_op jit(solution)/shard_map/reduce_scatter | solution.py:194
  211.4 37.6 %reduce-scatter.26.cloned.1.call-done = bf16[128,256]{1,0:T(8,128)(2,1)} async-done(((bf16[1024,256]{1,0:T(8,128)(2,1)}), bf16[128,256]{1,0:T(8,128)(2,1)}) %reduce-scatter.26.cloned.1.call-update) | async-done | bytes 65552
  250.7 40.4 %reduce-scatter.24.cloned.1.call-done = bf16[128,768]{1,0:T(8,128)(2,1)} async-done(((bf16[1024,768]{1,0:T(8,128)(2,1)}), bf16[128,768]{1,0:T(8,128)(2,1)}) %reduce-scatter.24.cloned.1.call-update) | async-done | bytes 196624
  293.2 42.7 %reduce-scatter.22.cloned.1.call-done = bf16[128,1024]{1,0:T(8,128)(2,1)} async-done(((bf16[1024,1024]{1,0:T(8,128)(2,1)}), bf16[128,1024]{1,0:T(8,128)(2,1)}) %reduce-scatter.22.cloned.1.call-update) | async-done | bytes 262160
  337.7 3.6 convolution_bitcast_fusion
  341.3 39.4 %psum.7 = f32[4,1024]{1,0:T(4,128)} all-reduce(f32[4,1024]{1,0:T(4,128)S(1)} %convolution_bitcast_fusion), channel_id=1, replica_groups=mesh['dp'=8,'mp'=4] {'dp','mp'}, use_global_device_ids=true, to_apply=%region_6.7 | all-reduce | flops 4096 | bytes 32768 | tf_op jit(solution)/shard_map/psum | solution.py:189
  380.7 3.1 fusion.24
  (85 shorter events, 36.8 us)
Async XLA Ops:
  7.2 14.0 %copy-start = (bf16[1024,1024]{1,0:T(8,128)(2,1)S(1)}, bf16[1024,1024]{1,0:T(8,128)(2,1)}, u32[]{:S(2)}) copy-start(bf16[1024,1024]{1,0:T(8,128)(2,1)} %param.20) | copy-start | bytes 6291460
  7.2 46.6 %all-gather.6.cloned.1.call-start = ((), (), s32[]{:S(2)}) async-start(), calls=%async_computation.12 | async-start | bytes 1310720 | tf_op jit(solution)/shard_map/all_gather | solution.py:82
  7.9 73.3 %all-gather.4.cloned.1.call-start = ((), (), s32[]{:S(2)}) async-start(), calls=%async_computation.7 | async-start | bytes 1310720 | tf_op jit(solution)/shard_map/all_gather | solution.py:81
  11.8 3.8 copy-start.12
  11.8 3.8 copy-start.10
  11.8 3.8 copy-start.11
  21.2 30.3 %copy-start.6 = (bf16[1,128,1024]{2,1,0:T(8,128)(2,1)S(1)}, bf16[1,128,1024]{2,1,0:T(8,128)(2,1)}, u32[]{:S(2)}) copy-start(bf16[1,128,1024]{2,1,0:T(8,128)(2,1)} %param.13) | copy-start | bytes 786436
  28.1 20.9 %collective-permute-start = (f32[128,1024]{1,0:T(8,128)S(1)}, f32[128,1024]{1,0:T(8,128)S(1)}, u32[]{:S(2)}, u32[]{:S(2)}) collective-permute-start(f32[128,1024]{1,0:T(8,128)S(1)} %get-tuple-element.57), channel_id=1, source_target_pairs={{0,1},{1,2},{2,3},{4,5},{5,6},{6,7},{8,9},{9,10},{10,11},{12,13},{... | collective-permute-start | bytes 1572872 | tf_op jit(solution)/shard_map/ppermute | solution.py:15
  33.0 18.4 %collective-permute-start.1 = (f32[128,1024]{1,0:T(8,128)S(1)}, f32[128,1024]{1,0:T(8,128)S(1)}, u32[]{:S(2)}, u32[]{:S(2)}) collective-permute-start(f32[128,1024]{1,0:T(8,128)S(1)} %get-tuple-element.58), channel_id=1, source_target_pairs={{1,0},{2,1},{3,2},{5,4},{6,5},{7,6},{9,8},{10,9},{11,10},{13,12},{... | collective-permute-start | bytes 1572872 | tf_op jit(solution)/shard_map/ppermute | solution.py:15
  53.5 93.7 %reduce-scatter.14.cloned.1.call-start = ((), (), s32[]{:S(2)}) async-start(), calls=%async_computation.8 | async-start | bytes 1310720 | tf_op jit(solution)/shard_map/reduce_scatter | solution.py:147
  113.1 7.3 %copy-start.7 = (bf16[1,512,256]{2,1,0:T(8,128)(2,1)}, bf16[1,512,256]{2,1,0:T(8,128)(2,1)S(1)}, u32[]{:S(2)}) copy-start(bf16[1,512,256]{2,1,0:T(8,128)(2,1)S(1)} %copy.45) | copy-start | bytes 786436
  116.8 31.5 %copy-start.4 = (bf16[1,128,1024]{2,1,0:T(8,128)(2,1)S(1)}, bf16[1,128,1024]{2,1,0:T(8,128)(2,1)}, u32[]{:S(2)}) copy-start(bf16[1,128,1024]{2,1,0:T(8,128)(2,1)} %param.23) | copy-start | bytes 786436
  120.5 90.9 %reduce-scatter.18.cloned.1.call-start = ((), (), s32[]{:S(2)}) async-start(), calls=%async_computation.10 | async-start | bytes 2359296 | tf_op jit(solution)/shard_map/reduce_scatter | solution.py:194
  149.6 15.1 %copy-start.5 = (bf16[128,1024]{1,0:T(8,128)(2,1)}, bf16[128,1024]{1,0:T(8,128)(2,1)S(1)}, u32[]{:S(2)}) copy-start(bf16[128,1024]{1,0:T(8,128)(2,1)S(1)} %fusion.41) | copy-start | bytes 786436
  149.6 7.0 %collective-permute-start.2 = (bf16[128,1024]{1,0:T(8,128)(2,1)S(1)}, bf16[128,1024]{1,0:T(8,128)(2,1)S(1)}, u32[]{:S(2)}, u32[]{:S(2)}) collective-permute-start(bf16[128,1024]{1,0:T(8,128)(2,1)S(1)} %fusion.41), channel_id=1, source_target_pairs={{0,1},{1,2},{2,3},{4,5},{5,6},{6,7},{8,9},{9,10},{10,11},{12,13},{... | collective-permute-start | bytes 786440 | tf_op jit(solution)/shard_map/ppermute | solution.py:23
  150.9 10.2 %collective-permute-start.3 = (bf16[128,1024]{1,0:T(8,128)(2,1)S(1)}, bf16[128,1024]{1,0:T(8,128)(2,1)S(1)}, u32[]{:S(2)}, u32[]{:S(2)}) collective-permute-start(bf16[128,1024]{1,0:T(8,128)(2,1)S(1)} %fusion.41), channel_id=1, source_target_pairs={{1,0},{2,1},{3,2},{5,4},{6,5},{7,6},{9,8},{10,9},{11,10},{13,12},{... | collective-permute-start | bytes 786440 | tf_op jit(solution)/shard_map/ppermute | solution.py:26
  170.6 78.4 %reduce-scatter.26.cloned.1.call-start = ((), (), s32[]{:S(2)}) async-start(), calls=%async_computation.15 | async-start | bytes 589824
  170.9 2.8 copy-start.3
  173.7 1.6 copy-start.8
  173.7 1.6 copy-start.9
  175.2 115.8 %reduce-scatter.24.cloned.1.call-start = ((), (), s32[]{:S(2)}) async-start(), calls=%async_computation.14 | async-start | bytes 1769472
  183.0 3.2 copy-start.13
  186.1 149.8 %reduce-scatter.22.cloned.1.call-start = ((), (), s32[]{:S(2)}) async-start(), calls=%async_computation.13 | async-start | bytes 2359296
  191.1 1.7 copy-start.1
  192.8 1.0 copy-start.2
  199.9 183.9 %reduce-scatter.20.cloned.1.call-start = ((), (), s32[]{:S(2)}) async-start(), calls=%async_computation.11 | async-start | bytes 327680 | tf_op jit(solution)/shard_map/reduce_scatter | solution.py:202
  211.3 174.0 %reduce-scatter.16.cloned.1.call-start = ((), (), s32[]{:S(2)}) async-start(), calls=%async_computation.9 | async-start | bytes 327680 | tf_op jit(solution)/shard_map/reduce_scatter | solution.py:199
Sparse Core Ops, SparseCore 0:
  9.6 32.7 all-gather.5
  53.7 27.5 all-gather.3
  120.6 26.6 reduce-scatter.13
  170.7 40.5 reduce-scatter.17
  214.8 34.1 reduce-scatter.25
  252.5 38.4 reduce-scatter.23
  294.7 41.1 reduce-scatter.21
  338.2 19.6 reduce-scatter.19
  360.2 17.9 reduce-scatter.15
where the time goes:
time: 395 us; the launch traced here: 393 us
  waiting for transfers between devices  211 us (53%)
  matrix products  76.2 us (19%)
  blocking collectives  39.4 us (10%)
  local copies, waits for them, and re-layouts  34.9 us (9%)
  between operations  14.8 us (4%)
  starting transfers between devices  9.64 us (2%)
  other arithmetic  7.31 us (2%)
    unnamed x12, waiting for transfers between devices  122 us
    psum x1, blocking collectives, shards(): sum_attr = lax.psum(dw_attr, ('dp', 'mp'))  39.4 us
    reduce_scatter x1, waiting for transfers between devices, shards(): lax.psum_scatter(jnp.einsum('ind,icd->nc', dqkv, w_qkv, preferred_element...  26.7 us
    all_gather x1, waiting for transfers between devices, shards(): lax.all_gather(normed, 'mp', axis=0, tiled=True)  25.6 us
    unnamed x38, local copies, waits for them, and re-layouts  20.7 us
    ppermute x2, waiting for transfers between devices, shifted(): return lax.ppermute(block, axis, route)  17.1 us
    reduce_scatter x1, waiting for transfers between devices, shards(): lax.psum_scatter(dw_out.astype(jnp.bfloat16), 'dp', scatter_dimension=0,...  11.3 us
    dot_general x1, matrix products, attend_block(): jnp.einsum('hqk,khd->qhd', dscore, keys, preferred_element_type=jnp.float32)  8.43 us
  transfers between devices with their start and end apart: 13, of which 10 were waited for; matrix products, arithmetic and copies ran while one was open for 16% of the time, Pallas kernels for 0%

commit v1 on v0

--- a/solution.py
+++ b/solution.py
@@ -1,6 +1,10 @@
+import functools
+
 import jax
 import jax.numpy as jnp
 from jax import lax
+from jax.experimental import pallas as pl
+from jax.experimental.pallas import tpu as pltpu
 from jax.sharding import PartitionSpec as P
 
 HDIM = 64
@@ -206,9 +210,594 @@
     return (d_grid[None], d_mesh[None], sum_attr, sum_in, sum_out, sum_qkv, sum_o)
 
 
+F32 = jnp.float32
+BF16 = jnp.bfloat16
+LANES = 128
+TILE = 256
+
+
+def nn(a, b):
+    return jnp.dot(a, b, preferred_element_type=F32)
+
+
+def nt(a, b):
+    return lax.dot_general(a, b, (((1,), (1,)), ((), ())), preferred_element_type=F32)
+
+
+def tn(a, b):
+    return lax.dot_general(a, b, (((0,), (0,)), ((), ())), preferred_element_type=F32)
+
+
+def span(index, size):
+    return pl.ds(pl.multiple_of(index * size, size), size)
+
+
+def loop(count, body):
+    def step(i, carry):
+        body(i)
+        return carry
+
+    lax.fori_loop(0, count, step, 0)
+
+
+def layer_kernel(
+    n_mp,
+    grid_ref,
+    mesh_ref,
+    icol_ref,
+    irow_ref,
+    aux_ref,
+    w_attr_ref,
+    w_in_ref,
+    w_out_ref,
+    w_qkv_ref,
+    w_o_ref,
+    cot_ref,
+    d_grid_ref,
+    d_mesh_ref,
+    d_attr_ref,
+    d_in_ref,
+    d_out_ref,
+    d_qkv_ref,
+    d_o_ref,
+    split_ref,
+    pre_ref,
+    hid_ref,
+    msg_ref,
+    hsend,
+    hrecv,
+    node_ref,
+    x_all,
+    cot_all,
+    qkvg,
+    dqkv,
+    att_ref,
+    dxs,
+    dxr,
+    beside,
+    dproj_ref,
+    parts,
+    r1,
+    r2,
+    r3,
+    mpb,
+    mpr,
+    at_own,
+    at_recv,
+    at_all,
+    cot_sem,
+    x_sem,
+    halo_sem,
+    dx_sem,
+    beside_sem,
+    rs_sem,
+    mp_sem,
+    at_sem,
+):
+    d = lax.axis_index("dp")
+    me = lax.axis_index("mp")
+    core = d % 2
+    px = (d // 2) % 2
+    py = d // 4
+    by_core = (d + 1 - 2 * core, me)
+    by_x = (d + 2 - 4 * px, me)
+    by_y = (d + 4 - 8 * py, me)
+    second = (by_x[0] * (1 - core) + by_y[0] * core, me)
+    third = (by_y[0] * (1 - core) + by_x[0] * core, me)
+
+    def along(offset):
+        return (d, (me + offset + n_mp) % n_mp)
+
+    grid_rows, c = grid_ref.shape
+    nodes = mesh_ref.shape[0]
+    edges = aux_ref.shape[0]
+    attrs = w_attr_ref.shape[0]
+    width = w_o_ref.shape[0]
+    total = nodes * n_mp
+    rows = parts.shape[3]
+    cols = mpb.shape[3]
+    scale = HDIM ** (-0.5)
+    chunks = edges // TILE
+
+    def copy(src, dst, sems, to):
+        return pltpu.make_async_remote_copy(
+            src_ref=src,
+            dst_ref=dst,
+            send_sem=sems.at[0],
+            recv_sem=sems.at[1],
+            device_id=to,
+            device_id_type=pl.DeviceIdType.MESH,
+        )
+
+    barrier = pltpu.get_barrier_semaphore()
+    greeted = [by_core, by_x, by_y] + [along(o) for o in range(1, n_mp)]
+    for other in greeted:
+        pl.semaphore_signal(
+            barrier, inc=1, device_id=other, device_id_type=pl.DeviceIdType.MESH
+        )
+    pl.semaphore_wait(barrier, len(greeted))
+
+    def block(o):
+        return pl.ds(o * nodes, nodes)
+
+    cot_copies = [
+        copy(cot_ref, cot_all.at[block(o)], cot_sem.at[o - 1], along(o)) for o in range(1, n_mp)
+    ]
+    for one in cot_copies:
+        one.start()
+    cot_all[block(0), :] = cot_ref[...]
+
+    def project(j):
+        at = span(j, 2 * TILE)
+        value = nn(grid_ref[...], w_in_ref[:, at])
+        high = value.astype(BF16)
+        split_ref[pl.ds(0, grid_rows), at] = high
+        split_ref[pl.ds(grid_rows, grid_rows), at] = (value - high.astype(F32)).astype(BF16)
+
+    loop(c // (2 * TILE), project)
+
+    def edge_forward(i):
+        at = span(i, TILE)
+        source = icol_ref[at, 0:1]
+        place = lax.broadcasted_iota(jnp.int32, (TILE, grid_rows), 1)
+        table = (source == place).astype(F32).astype(BF16)
+        table = jnp.concatenate([table, table], axis=1)
+        aux = aux_ref[at, :]
+        pre = nn(table, split_ref[...])
+        for a in range(attrs):
+            pre = pre + aux[:, a : a + 1] * w_attr_ref[a : a + 1, :]
+        pre_ref[at, :] = pre
+        hidden = (pre / (1.0 + jnp.exp(-pre)) * aux[:, attrs : attrs + 1]).astype(BF16)
+        hid_ref[at, :] = hidden
+        msg_ref[at, :] = nn(hidden, w_out_ref[...]).astype(BF16)
+
+    loop(chunks, edge_forward)
+
+    dest = irow_ref[1:2, :]
+    place = lax.broadcasted_iota(jnp.int32, (2 * nodes, edges), 0)
+    place = jnp.where(place < nodes, place, place + nodes)
+    sides = nn((dest == place).astype(F32).astype(BF16), msg_ref[...])
+    hsend[0] = sides[:nodes].astype(BF16)
+    hsend[1] = sides[nodes:].astype(BF16)
+    down = copy(hsend.at[0], hrecv.at[1], halo_sem.at[0], along(-1))
+    up = copy(hsend.at[1], hrecv.at[0], halo_sem.at[1], along(1))
+    first, last = me == 0, me == n_mp - 1
+
+    def exchange(lower, upper, low_slot, high_slot):
+        @pl.when(jnp.logical_not(first))
+        def _():
+            lower.start()
+
+        @pl.when(jnp.logical_not(last))
+        def _():
+            upper.start()
+
+        @pl.when(first)
+        def _():
+            low_slot[...] = jnp.zeros_like(low_slot)
+
+        @pl.when(last)
+        def _():
+            high_slot[...] = jnp.zeros_like(high_slot)
+
+    def settle(lower, upper):
+        @pl.when(jnp.logical_not(first))
+        def _():
+            lower.wait_send()
+            upper.wait_recv()
+
+        @pl.when(jnp.logical_not(last))
+        def _():
+            upper.wait_send()
+            lower.wait_recv()
+
+    exchange(down, up, hrecv.at[0], hrecv.at[1])
+    place = lax.broadcasted_iota(jnp.int32, (nodes, edges), 0) + nodes
+    node = mesh_ref[...].astype(F32) + nn(
+        (dest == place).astype(F32).astype(BF16), msg_ref[...]
+    )
+    settle(down, up)
+    node = node + hrecv[0].astype(F32) + hrecv[1].astype(F32)
+    inv = lax.rsqrt(jnp.mean(node * node, axis=-1, keepdims=True) + EPS)
+    node_ref[...] = node
+    x_all[block(0), :] = (node * inv).astype(BF16)
+
+    x_copies = [
+        copy(x_all.at[block(0)], x_all.at[block(o)], x_sem.at[o - 1], along(o))
+        for o in range(1, n_mp)
+    ]
+    for one in x_copies:
+        one.start()
+
+    def qkv(o):
+        band = x_all[block(o), :]
+        for i in range(3):
+            qkvg[i, block(o), :] = nn(band, w_qkv_ref[i]).astype(BF16)
+
+    qkv(0)
+    for one in cot_copies:
+        one.wait()
+    qkvg[3] = nt(cot_all[...], w_o_ref[...]).astype(BF16)
+    nearest = sorted(range(1, n_mp), key=lambda o: min(o, n_mp - o))
+    for o in nearest:
+        x_copies[o - 1].wait()
+        qkv(o)
+
+    lane = lax.broadcasted_iota(jnp.int32, (1, LANES), 1)
+
+    def heads(p):
+        at = span(p, LANES)
+        q, k, v, g = (qkvg[i, :, at] for i in range(4))
+        sums = [jnp.zeros((total, LANES), F32) for _ in range(4)]
+        for h in range(LANES // HDIM):
+            own = jnp.logical_and(lane >= h * HDIM, lane < (h + 1) * HDIM)
+            own = own.astype(F32).astype(BF16)
+            qh, kh, vh, gh = q * own, k * own, v * own, g * own
+            scores = nt(qh, k) * scale
+            probs = jnp.exp(scores - jnp.max(scores, axis=-1, keepdims=True))
+            probs = probs * (1.0 / jnp.sum(probs, axis=-1, keepdims=True))
+            probs_b = probs.astype(BF16)
+            dprob = nt(gh, v)
+            delta = jnp.sum(probs * dprob, axis=-1, keepdims=True)
+            dscore = (probs * (dprob - delta) * scale).astype(BF16)
+            sums[0] = sums[0] + nn(dscore, kh)
+            sums[1] = sums[1] + tn(dscore, qh)
+            sums[2] = sums[2] + tn(probs_b, gh)
+            sums[3] = sums[3] + nn(probs_b, vh)
+        for i in range(3):
+            dqkv[i, :, at] = sums[i].astype(BF16)
+        att_ref[:, at] = sums[3].astype(BF16)
+
+    loop(width // LANES, heads)
+
+    dx_copies = [
+        copy(dxs.at[block(o)], dxr.at[o - 1], dx_sem.at[o - 1], along(-o)) for o in range(1, n_mp)
+    ]
+    half = n_mp // 2
+    for start in (half, 0):
+        at = pl.ds(start * nodes, half * nodes)
+        value = nt(dqkv[0, at, :], w_qkv_ref[0])
+        value = value + nt(dqkv[1, at, :], w_qkv_ref[1])
+        value = value + nt(dqkv[2, at, :], w_qkv_ref[2])
+        dxs[at, :] = value.astype(BF16)
+        for o in range(max(start, 1), start + half):
+            dx_copies[o - 1].start()
+
+    def keep(j):
+        return (j * 2 + px) * (1 - core) + (py * 2 + j) * core
+
+    def give(j):
+        return (j * 2 + 1 - px) * (1 - core) + ((1 - py) * 2 + j) * core
+
+    def stage(group, number):
+        sems = rs_sem.at[group]
+        mine = parts.at[group]
+        if number == 0:
+            return [copy(mine.at[1 - core], r1.at[group], sems.at[0], by_core)]
+        if number == 1:
+            return [
+                copy(mine.at[core, give(j)], r2.at[group, j], sems.at[1 + j], second)
+                for j in range(2)
+            ]
+        rest = (1 - py) * (1 - core) + (1 - px) * core
+        return [copy(mine.at[core, keep(rest)], r3.at[group], sems.at[3], third)]
+
+    def begin(group, number):
+        for one in stage(group, number):
+            one.start()
+
+    def add(group, slot, other):
+        value = parts[group, core, slot].astype(F32) + other.astype(F32)
+        parts[group, core, slot] = value.astype(BF16)
+
+    def finish_first(group):
+        for one in stage(group, 0):
+            one.wait()
+        for j in range(2):
+            add(group, give(j), r1[group, give(j)])
+        begin(group, 1)
+        for j in range(2):
+            add(group, keep(j), r1[group, keep(j)])
+
+    def finish_second(group):
+        for one in stage(group, 1):
+            one.wait()
+        rest = (1 - py) * (1 - core) + (1 - px) * core
+        add(group, keep(rest), r2[group, rest])
+        begin(group, 2)
+        add(group, keep(1 - rest), r2[group, 1 - rest])
+
+    def finish_third(group):
+        for one in stage(group, 2):
+            one.wait()
+        return parts[group, core, py * 2 + px].astype(F32) + r3[group].astype(F32)
+
+    def pairs(fill):
+        loop(parts.shape[2], fill)
+
+    def fill_qkv(j):
+        at = span(j, 2 * rows)
+        x_part = x_all[:, at]
+        for i in range(3):
+            value = tn(x_part, dqkv[i]).astype(BF16)
+            for side in range(2):
+                parts[0, side, j, :, pl.ds(i * width, width)] = value[side * rows : (side + 1) * rows]
+        value = tn(cot_all[:, at], att_ref[...]).astype(BF16)
+        for side in range(2):
+            parts[0, side, j, :, pl.ds(3 * width, width)] = value[side * rows : (side + 1) * rows]
+
+    pairs(fill_qkv)
+    begin(0, 0)
+
+    for one in dx_copies:
+        one.wait()
+    dx = dxs[block(0), :].astype(F32)
+    for o in range(1, n_mp):
+        dx = dx + dxr[o - 1].astype(F32)
+    node = node_ref[...]
+    inv = lax.rsqrt(jnp.mean(node * node, axis=-1, keepdims=True) + EPS)
+    mean = jnp.mean(dx * node, axis=-1, keepdims=True)
+    dnode = cot_ref[...].astype(F32) + inv * dx - node * inv * inv * inv * mean
+    beside[pl.ds(nodes, nodes), :] = dnode.astype(BF16)
+    middle = beside.at[pl.ds(nodes, nodes)]
+    low, high = beside.at[pl.ds(0, nodes)], beside.at[pl.ds(2 * nodes, nodes)]
+    down = copy(middle, high, beside_sem.at[0], along(-1))
+    up = copy(middle, low, beside_sem.at[1], along(1))
+    exchange(down, up, low, high)
+    d_mesh_ref[...] = dnode.astype(BF16)
+    finish_first(0)
+    settle(down, up)
+
+    def edge_gather(i):
+        at = span(i, TILE)
+        place = lax.broadcasted_iota(jnp.int32, (TILE, 3 * nodes), 1)
+        table = (icol_ref[at, 1:2] == place).astype(F32) * aux_ref[at, attrs : attrs + 1]
+        msg_ref[at, :] = nn(table.astype(BF16), beside[...]).astype(BF16)
+
+    loop(chunks, edge_gather)
+
+    def fill_out(j):
+        value = tn(hid_ref[:, span(j, 2 * rows)], msg_ref[...]).astype(BF16)
+        for side in range(2):
+            parts[1, side, j] = value[side * rows : (side + 1) * rows]
+
+    pairs(fill_out)
+    begin(1, 0)
+    finish_second(0)
+
+    at_own[...] = jnp.zeros_like(at_own)
+
+    def edge_backward(i):
+        at = span(i, TILE)
+        aux = aux_ref[at, :]
+        pre = pre_ref[at, :]
+        sigma = 1.0 / (1.0 + jnp.exp(-pre))
+        dpre = nt(msg_ref[at, :], w_out_ref[...])
+        dpre = dpre * sigma * (1.0 + pre * (1.0 - sigma)) * aux[:, attrs : attrs + 1]
+        for a in range(attrs):
+            at_own[a : a + 1, :] += jnp.sum(aux[:, a : a + 1] * dpre, axis=0, keepdims=True)
+        msg_ref[at, :] = dpre.astype(BF16)
+
+    loop(chunks, edge_backward)
+    finish_first(1)
+
+    attr_steps = [
+        copy(at_own, at_recv.at[i], at_sem.at[i], to) for i, to in enumerate((by_core, by_x, by_y))
+    ]
+    attr_steps[0].start()
+    place = lax.broadcasted_iota(jnp.int32, (grid_rows, edges), 0)
+    table = (irow_ref[0:1, :] == place).astype(F32).astype(BF16)
+    dproj_ref[...] = nn(table, msg_ref[...]).astype(BF16)
+
+    def fill_in(j):
+        value = tn(grid_ref[:, span(j, 2 * rows)], dproj_ref[...]).astype(BF16)
+        for side in range(2):
+            parts[2, side, j] = value[side * rows : (side + 1) * rows]
+
+    pairs(fill_in)
+    begin(2, 0)
+    finish_second(1)
+    attr_steps[0].wait()
+    at_own[...] = at_own[...] + at_recv[0]
+    attr_steps[1].start()
+
+    def grid_back(j):
+        at = span(j, 2 * TILE)
+        d_grid_ref[:, at] = nt(dproj_ref[...], w_in_ref[at, :]).astype(BF16)
+
+    finish_first(2)
+    loop(c // (2 * TILE), grid_back)
+
+    value = finish_third(0)
+    for i in range(3):
+        d_qkv_ref[i] = value[:, i * width : (i + 1) * width]
+    d_o_ref[...] = value[:, 3 * width :].T
+    attr_steps[1].wait()
+    at_own[...] = at_own[...] + at_recv[1]
+    attr_steps[2].start()
+
+    def spread(group):
+        value = finish_third(group)
+        for t in range(n_mp):
+            mpb[group - 1, t] = value[:, t * cols : (t + 1) * cols].astype(BF16)
+        copies = [
+            copy(
+                mpb.at[group - 1, (me + o) % n_mp],
+                mpr.at[group - 1, o - 1],
+                mp_sem.at[group - 1, o - 1],
+                along(o),
+            )
+            for o in range(1, n_mp)
+        ]
+        for one in copies:
+            one.start()
+        return copies
+
+    def collect(group, copies, out_ref):
+        for one in copies:
+            one.wait()
+        value = mpb[group - 1, me].astype(F32)
+        for o in range(1, n_mp):
+            value = value + mpr[group - 1, o - 1].astype(F32)
+        out_ref[...] = value
+
+    out_copies = spread(1)
+    finish_second(2)
+    attr_steps[2].wait()
+    at_all[0] = at_own[...] + at_recv[2]
+    attr_copies = [
+        copy(at_all.at[0], at_all.at[o], at_sem.at[2 + o], along(o)) for o in range(1, n_mp)
+    ]
+    for one in attr_copies:
+        one.start()
+    in_copies = spread(2)
+    for one in attr_copies:
+        one.wait()
+    value = at_all[me]
+    for s in range(1, n_mp):
+        value = value + at_all[(me + n_mp - s) % n_mp]
+    d_attr_ref[...] = value
+    collect(1, out_copies, d_out_ref)
+    collect(2, in_copies, d_in_ref)
+
+
+def fused(
+    grid_latent,
+    mesh_latent,
+    edge_source,
+    edge_dest,
+    edge_count,
+    edge_attr,
+    w_attr,
+    w_in,
+    w_out,
+    w_qkv,
+    w_o,
+    cotangent,
+):
+    n_dp, n_mp = lax.axis_size("dp"), lax.axis_size("mp")
+    band = lax.axis_index("mp")
+    grid_rows, c = grid_latent.shape[1:]
+    nodes = mesh_latent.shape[1]
+    edges = edge_source.shape[1]
+    attrs = w_attr.shape[0]
+    width = w_qkv.shape[2]
+    total = nodes * n_mp
+    rows, cols = c // n_dp, c // n_mp
+    live = (jnp.arange(edges, dtype=jnp.int32) < edge_count[0, 0]).astype(F32)
+    irow = jnp.concatenate([edge_source - band * grid_rows, edge_dest - (band - 1) * nodes], axis=0)
+    aux = jnp.concatenate([edge_attr[0], live[None]], axis=0).T
+    vmem = pl.BlockSpec(memory_space=pltpu.VMEM)
+    shape = jax.ShapeDtypeStruct
+    dma = pltpu.SemaphoreType.DMA
+    outs = pl.pallas_call(
+        functools.partial(layer_kernel, n_mp),
+        out_shape=(
+            shape((grid_rows, c), BF16),
+            shape((nodes, c), BF16),
+            shape((attrs, c), F32),
+            shape((rows, cols), F32),
+            shape((rows, cols), F32),
+            shape((3, rows, width), F32),
+            shape((width, rows), F32),
+        ),
+        in_specs=[vmem] * 11,
+        out_specs=[vmem] * 7,
+        scratch_shapes=[
+            pltpu.VMEM((2 * grid_rows, c), BF16),
+            pltpu.VMEM((edges, c), F32),
+            pltpu.VMEM((edges, c), BF16),
+            pltpu.VMEM((edges, c), BF16),
+            pltpu.VMEM((2, nodes, c), BF16),
+            pltpu.VMEM((2, nodes, c), BF16),
+            pltpu.VMEM((nodes, c), F32),
+            pltpu.VMEM((total, c), BF16),
+            pltpu.VMEM((total, c), BF16),
+            pltpu.VMEM((4, total, width), BF16),
+            pltpu.VMEM((3, total, width), BF16),
+            pltpu.VMEM((total, width), BF16),
+            pltpu.VMEM((total, c), BF16),
+            pltpu.VMEM((n_mp - 1, nodes, c), BF16),
+            pltpu.VMEM((3 * nodes, c), BF16),
+            pltpu.VMEM((grid_rows, c), BF16),
+            pltpu.VMEM((3, 2, n_dp // 2, rows, c), BF16),
+            pltpu.VMEM((3, n_dp // 2, rows, c), BF16),
+            pltpu.VMEM((3, 2, rows, c), BF16),
+            pltpu.VMEM((3, rows, c), BF16),
+            pltpu.VMEM((2, n_mp, rows, cols), BF16),
+            pltpu.VMEM((2, n_mp - 1, rows, cols), BF16),
+            pltpu.VMEM((attrs, c), F32),
+            pltpu.VMEM((3, attrs, c), F32),
+            pltpu.VMEM((n_mp, attrs, c), F32),
+            dma((n_mp - 1, 2)),
+            dma((n_mp - 1, 2)),
+            dma((2, 2)),
+            dma((n_mp - 1, 2)),
+            dma((2, 2)),
+            dma((3, 4, 2)),
+            dma((2, n_mp - 1, 2)),
+            dma((2 + n_mp, 2)),
+        ],
+        compiler_params=pltpu.CompilerParams(
+            collective_id=0, has_side_effects=True, vmem_limit_bytes=58 * 2**20
+        ),
+    )(
+        grid_latent[0],
+        mesh_latent[0],
+        irow.T,
+        irow,
+        aux,
+        w_attr,
+        w_in,
+        w_out,
+        w_qkv,
+        w_o,
+        cotangent[0],
+    )
+    return (outs[0][None], outs[1][None]) + tuple(outs[2:])
+
+
+def step(*arrays):
+    grid_latent, mesh_latent, edge_source, w_qkv = (arrays[i] for i in (0, 1, 2, 9))
+    c, width = w_qkv.shape[1:]
+    n_dp, n_mp = lax.axis_size("dp"), lax.axis_size("mp")
+    fits = (
+        n_dp == 8
+        and n_mp % 2 == 0
+        and n_mp * mesh_latent.shape[1] <= 512
+        and 4 * width == c
+        and width % LANES == 0
+        and c % (2 * TILE) == 0
+        and (c // n_dp) % LANES == 0
+        and edge_source.shape[1] % TILE == 0
+        and grid_latent.shape[1] % LANES == 0
+    )
+    return fused(*arrays) if fits else shards(*arrays)
+
+
 def solution(mesh):
     return jax.shard_map(
-        shards,
+        step,
         mesh=mesh,
         in_specs=(
             P("dp", "mp", None),

time: 395 us -> 153 us (0.39)
  waiting for transfers between devices: 211 us -> 0 us
  Pallas kernels: 0 us -> 138 us
  matrix products: 76.2 us -> 0 us
  blocking collectives: 39.4 us -> 0 us
  local copies, waits for them, and re-layouts: 34.9 us -> 11.3 us
  between operations: 14.8 us -> 1.32 us
  starting transfers between devices: 9.64 us -> 0 us
  other arithmetic: 7.31 us -> 2.04 us
    pallas_call x0 -> x1, Pallas kernels: none -> 138 us  [fused(): pl.pallas_call(functools.partial(layer_kernel, n_mp), out_shape=(shape((g...]
    unnamed x12 -> x0, waiting for transfers between devices: 122 us -> none
    dot_general x19 -> x0, matrix products: 71.8 us -> none  [the longest x1 8.43 us: attend_block(): jnp.einsum('hqk,khd->qhd', dscore, keys, preferred_element_type=jnp.float32)]
    psum x1 -> x0, blocking collectives: 39.4 us -> none  [shards(): sum_attr = lax.psum(dw_attr, ('dp', 'mp'))]
    reduce_scatter x4 -> x0, waiting for transfers between devices: 38.1 us -> none  [the longest x1 26.7 us: shards(): lax.psum_scatter(jnp.einsum('ind,icd->nc', dqkv, w_qkv, preferred_element...]
    ppermute x4 -> x0, waiting for transfers between devices: 26 us -> none  [the longest x2 17.1 us: shifted(): return lax.ppermute(block, axis, route)]
    all_gather x2 -> x0, waiting for transfers between devices: 25.6 us -> none  [the longest x1 25.6 us: shards(): lax.all_gather(normed, 'mp', axis=0, tiled=True)]
    unnamed x38 -> x11, local copies, waits for them, and re-layouts: 20.7 us -> 9.46 us
  transfers between devices with their start and end apart: 13 -> 0, of which waited for: 10 -> 0; matrix products, arithmetic and copies ran while one was open for 16% -> 0% of each run, Pallas kernels for 0% -> 0%
where the time goes in v1:
time: 153 us; the launch traced here: 152 us
  Pallas kernels  138 us (90%)
  local copies, waits for them, and re-layouts  11.3 us (7%)
  other arithmetic  2.04 us (1%)
    pallas_call x1, Pallas kernels, fused(): pl.pallas_call(functools.partial(layer_kernel, n_mp), out_shape=(shape((g...  138 us
    unnamed x11, local copies, waits for them, and re-layouts  9.46 us

profile of v1, /device:TPU:0, one launch (start us, length us, event | category | flops | bytes accessed | tf_op | source)
XLA Modules:
  0.0 152.3 jit_solution(18334119704897058120)
XLA Ops:
  1.3 0.7 broadcast_subtract_fusion
  2.0 0.6 pad_add_fusion
  2.6 0.7 pad_maximum_fusion
  3.3 0.9 copy.21
  4.3 0.9 copy.22.icol_ref
  5.2 137.6 %shard_map.171 = (bf16[256,1024]{1,0:T(8,128)(2,1)}, bf16[128,1024]{1,0:T(8,128)(2,1)}, f32[4,1024]{1,0:T(4,128)}, f32[128,256]{1,0:T(8,128)}, f32[128,256]{1,0:...) custom-call(bf16[256,1024]{1,0:T(8,128)(2,1)} %bitcast.12, bf16[128,1024]{1,0:T(8,128)(2,1)} %bitcast.14, ...), custom_call_target="tpu_custom_call" | custom-call | tf_op jit(solution)/shard_map/pallas_call | solution.py:713
  142.9 0.0 copy-start
  142.9 0.0 copy-start.1
  142.9 1.9 %copy.31 = bf16[1,256,1024]{2,1,0:T(8,128)(2,1)} copy(bf16[1,256,1024]{2,1,0:T(8,128)(2,1)} %bitcast.13) | data formatting | bytes 1048576
  144.8 1.7 %copy.32 = bf16[1,128,1024]{2,1,0:T(8,128)(2,1)} copy(bf16[1,128,1024]{2,1,0:T(8,128)(2,1)} %bitcast.16) | data formatting | bytes 524288
  146.5 1.3 copy.33
  147.8 1.6 %copy.34 = f32[128,256]{1,0:T(8,128)} copy(f32[128,256]{1,0:T(8,128)} %get-tuple-element.35) | data formatting | bytes 262144
  149.4 1.6 %copy.35 = f32[128,256]{1,0:T(8,128)} copy(f32[128,256]{1,0:T(8,128)} %get-tuple-element.36) | data formatting | bytes 262144
  150.9 0.0 copy-done
  150.9 0.7 copy.36
  151.7 0.0 copy-done.1
  151.7 0.7 copy.37
  (1 shorter events, 0.0 us)
Async XLA Ops:
  142.9 8.1 %copy-start = (f32[3,128,256]{2,1,0:T(8,128)S(1)}, f32[3,128,256]{2,1,0:T(8,128)}, u32[]{:S(2)}) copy-start(f32[3,128,256]{2,1,0:T(8,128)} %get-tuple-element.37) | copy-start | bytes 1179652
  142.9 8.8 %copy-start.1 = (f32[256,128]{1,0:T(8,128)S(1)}, f32[256,128]{1,0:T(8,128)}, u32[]{:S(2)}) copy-start(f32[256,128]{1,0:T(8,128)} %get-tuple-element.38) | copy-start | bytes 393220

commit v2 on v1

--- a/solution.py
+++ b/solution.py
@@ -244,9 +244,10 @@
     n_mp,
     grid_ref,
     mesh_ref,
-    icol_ref,
-    irow_ref,
-    aux_ref,
+    source_ref,
+    dest_ref,
+    count_ref,
+    attr_ref,
     w_attr_ref,
     w_in_ref,
     w_out_ref,
@@ -261,9 +262,13 @@
     d_qkv_ref,
     d_o_ref,
     split_ref,
-    pre_ref,
+    slope_ref,
     hid_ref,
+    hid_t,
+    grid_t,
     msg_ref,
+    row_ref,
+    col_ref,
     hsend,
     hrecv,
     node_ref,
@@ -310,7 +315,7 @@
 
     grid_rows, c = grid_ref.shape
     nodes = mesh_ref.shape[0]
-    edges = aux_ref.shape[0]
+    edges = source_ref.shape[1]
     attrs = w_attr_ref.shape[0]
     width = w_o_ref.shape[0]
     total = nodes * n_mp
@@ -340,12 +345,74 @@
     def block(o):
         return pl.ds(o * nodes, nodes)
 
-    cot_copies = [
-        copy(cot_ref, cot_all.at[block(o)], cot_sem.at[o - 1], along(o)) for o in range(1, n_mp)
-    ]
-    for one in cot_copies:
-        one.start()
+    first, last = me == 0, me == n_mp - 1
+
+    def relay(blocks, sems):
+        def right(t):
+            return copy(blocks.at[block(t)], blocks.at[block(t + 1)], sems.at[0, t], along(1))
+
+        def left(t):
+            return copy(
+                blocks.at[block((n_mp - t) % n_mp)],
+                blocks.at[block(n_mp - t - 1)],
+                sems.at[1, t],
+                along(-1),
+            )
+
+        def send(t):
+            @pl.when(jnp.logical_and(me >= t, jnp.logical_not(last)))
+            def _():
+                right(t).start()
+
+            @pl.when(jnp.logical_and(me + t <= n_mp - 1, jnp.logical_not(first)))
+            def _():
+                left(t).start()
+
+        def hop(t, use=None):
+            @pl.when(me >= t)
+            def _():
+                right(t - 1).wait_recv()
+
+            @pl.when(me + t <= n_mp - 1)
+            def _():
+                left(t - 1).wait_recv()
+
+            if t < n_mp - 1:
+                send(t)
+            if use is not None:
+
+                @pl.when(me >= t)
+                def _():
+                    use(t)
+
+                @pl.when(me + t <= n_mp - 1)
+                def _():
+                    use(n_mp - t)
+
+        def drain():
+            for t in range(n_mp - 1):
+
+                @pl.when(jnp.logical_and(me >= t, jnp.logical_not(last)))
+                def _(t=t):
+                    right(t).wait_send()
+
+                @pl.when(jnp.logical_and(me + t <= n_mp - 1, jnp.logical_not(first)))
+                def _(t=t):
+                    left(t).wait_send()
+
+        return send, hop, drain
+
     cot_all[block(0), :] = cot_ref[...]
+    cot_send, cot_hop, cot_drain = relay(cot_all, cot_sem)
+    cot_send(0)
+
+    row_ref[...] = jnp.zeros_like(row_ref)
+    row_ref[0:1, :] = (source_ref[...] - me * grid_rows).astype(F32)
+    row_ref[1:2, :] = (dest_ref[...] - (me - 1) * nodes).astype(F32)
+    position = lax.broadcasted_iota(jnp.int32, (1, edges), 1)
+    row_ref[2:3, :] = (position < count_ref[...]).astype(F32)
+    row_ref[3 : 3 + attrs, :] = attr_ref[...]
+    col_ref[...] = row_ref[...].T
 
     def project(j):
         at = span(j, 2 * TILE)
@@ -358,22 +425,28 @@
 
     def edge_forward(i):
         at = span(i, TILE)
-        source = icol_ref[at, 0:1]
+        aux = col_ref[at, :]
         place = lax.broadcasted_iota(jnp.int32, (TILE, grid_rows), 1)
-        table = (source == place).astype(F32).astype(BF16)
+        table = (aux[:, 0:1].astype(jnp.int32) == place).astype(F32).astype(BF16)
         table = jnp.concatenate([table, table], axis=1)
-        aux = aux_ref[at, :]
         pre = nn(table, split_ref[...])
         for a in range(attrs):
-            pre = pre + aux[:, a : a + 1] * w_attr_ref[a : a + 1, :]
-        pre_ref[at, :] = pre
-        hidden = (pre / (1.0 + jnp.exp(-pre)) * aux[:, attrs : attrs + 1]).astype(BF16)
+            pre = pre + aux[:, 3 + a : 4 + a] * w_attr_ref[a : a + 1, :]
+        sigma = 1.0 / (1.0 + jnp.exp(-pre))
+        live = aux[:, 2:3]
+        slope_ref[at, :] = sigma * (1.0 + pre * (1.0 - sigma)) * live
+        hidden = (pre * sigma * live).astype(BF16)
         hid_ref[at, :] = hidden
         msg_ref[at, :] = nn(hidden, w_out_ref[...]).astype(BF16)
 
-    loop(chunks, edge_forward)
-
-    dest = irow_ref[1:2, :]
+    for i in range(chunks):
+        edge_forward(i)
+        if i + 1 < n_mp:
+            cot_hop(i + 1)
+    for t in range(chunks + 1, n_mp):
+        cot_hop(t)
+
+    dest = dest_ref[...] - (me - 1) * nodes
     place = lax.broadcasted_iota(jnp.int32, (2 * nodes, edges), 0)
     place = jnp.where(place < nodes, place, place + nodes)
     sides = nn((dest == place).astype(F32).astype(BF16), msg_ref[...])
@@ -381,8 +454,6 @@
     hsend[1] = sides[nodes:].astype(BF16)
     down = copy(hsend.at[0], hrecv.at[1], halo_sem.at[0], along(-1))
     up = copy(hsend.at[1], hrecv.at[0], halo_sem.at[1], along(1))
-    first, last = me == 0, me == n_mp - 1
-
     def exchange(lower, upper, low_slot, high_slot):
         @pl.when(jnp.logical_not(first))
         def _():
@@ -422,12 +493,8 @@
     node_ref[...] = node
     x_all[block(0), :] = (node * inv).astype(BF16)
 
-    x_copies = [
-        copy(x_all.at[block(0)], x_all.at[block(o)], x_sem.at[o - 1], along(o))
-        for o in range(1, n_mp)
-    ]
-    for one in x_copies:
-        one.start()
+    x_send, x_hop, x_drain = relay(x_all, x_sem)
+    x_send(0)
 
     def qkv(o):
         band = x_all[block(o), :]
@@ -435,53 +502,84 @@
             qkvg[i, block(o), :] = nn(band, w_qkv_ref[i]).astype(BF16)
 
     qkv(0)
-    for one in cot_copies:
-        one.wait()
+    cot_drain()
     qkvg[3] = nt(cot_all[...], w_o_ref[...]).astype(BF16)
-    nearest = sorted(range(1, n_mp), key=lambda o: min(o, n_mp - o))
-    for o in nearest:
-        x_copies[o - 1].wait()
-        qkv(o)
+
+    def turn(j):
+        at = span(j, TILE)
+        hid_t[at, :] = hid_ref[:, at].T
+        grid_t[at, :] = grid_ref[:, at].T
+
+    loop(c // TILE, turn)
+    for t in range(1, n_mp):
+        x_hop(t, qkv)
+    x_drain()
 
     lane = lax.broadcasted_iota(jnp.int32, (1, LANES), 1)
 
     def heads(p):
         at = span(p, LANES)
         q, k, v, g = (qkvg[i, :, at] for i in range(4))
-        sums = [jnp.zeros((total, LANES), F32) for _ in range(4)]
+        sums = [0.0] * 4
         for h in range(LANES // HDIM):
             own = jnp.logical_and(lane >= h * HDIM, lane < (h + 1) * HDIM)
             own = own.astype(F32).astype(BF16)
             qh, kh, vh, gh = q * own, k * own, v * own, g * own
-            scores = nt(qh, k) * scale
-            probs = jnp.exp(scores - jnp.max(scores, axis=-1, keepdims=True))
-            probs = probs * (1.0 / jnp.sum(probs, axis=-1, keepdims=True))
+            scores = nt(kh, q) * scale
+            probs = jnp.exp(scores - jnp.max(scores, axis=0, keepdims=True))
+            probs = probs * (1.0 / jnp.sum(probs, axis=0, keepdims=True))
             probs_b = probs.astype(BF16)
-            dprob = nt(gh, v)
-            delta = jnp.sum(probs * dprob, axis=-1, keepdims=True)
+            dprob = nt(vh, g)
+            delta = jnp.sum(probs * dprob, axis=0, keepdims=True)
             dscore = (probs * (dprob - delta) * scale).astype(BF16)
-            sums[0] = sums[0] + nn(dscore, kh)
-            sums[1] = sums[1] + tn(dscore, qh)
-            sums[2] = sums[2] + tn(probs_b, gh)
-            sums[3] = sums[3] + nn(probs_b, vh)
-        for i in range(3):
-            dqkv[i, :, at] = sums[i].astype(BF16)
-        att_ref[:, at] = sums[3].astype(BF16)
+            sums[0] = sums[0] + tn(kh, dscore)
+            sums[1] = sums[1] + nn(dscore, qh)
+            sums[2] = sums[2] + nn(probs_b, gh)
+            sums[3] = sums[3] + tn(vh, probs_b)
+        dqkv[0, :, at] = sums[0].T.astype(BF16)
+        dqkv[1, :, at] = sums[1].astype(BF16)
+        dqkv[2, :, at] = sums[2].astype(BF16)
+        att_ref[:, at] = sums[3].T.astype(BF16)
 
     loop(width // LANES, heads)
 
-    dx_copies = [
-        copy(dxs.at[block(o)], dxr.at[o - 1], dx_sem.at[o - 1], along(-o)) for o in range(1, n_mp)
-    ]
-    half = n_mp // 2
-    for start in (half, 0):
-        at = pl.ds(start * nodes, half * nodes)
-        value = nt(dqkv[0, at, :], w_qkv_ref[0])
-        value = value + nt(dqkv[1, at, :], w_qkv_ref[1])
-        value = value + nt(dqkv[2, at, :], w_qkv_ref[2])
-        dxs[at, :] = value.astype(BF16)
-        for o in range(max(start, 1), start + half):
-            dx_copies[o - 1].start()
+    value = nt(dqkv[0], w_qkv_ref[0])
+    value = value + nt(dqkv[1], w_qkv_ref[1])
+    value = value + nt(dqkv[2], w_qkv_ref[2])
+    dxs[...] = value.astype(BF16)
+
+    def right_sum(k):
+        return copy(dxs.at[block(n_mp - k)], dxr.at[0, k - 1], dx_sem.at[0, k - 1], along(1))
+
+    def left_sum(k):
+        return copy(dxs.at[block(k)], dxr.at[1, k - 1], dx_sem.at[1, k - 1], along(-1))
+
+    def pass_on(k):
+        def add_in(way, slot):
+            held = dxs[block(slot), :].astype(F32) + dxr[way, k].astype(F32)
+            dxs[block(slot), :] = held.astype(BF16)
+
+        @pl.when(me + k <= n_mp - 1)
+        def _():
+            if k < n_mp - 1:
+
+                @pl.when(jnp.logical_not(first))
+                def _():
+                    right_sum(k + 1).wait_recv()
+                    add_in(0, n_mp - k)
+
+            right_sum(k).start()
+
+        @pl.when(me >= k)
+        def _():
+            if k < n_mp - 1:
+
+                @pl.when(jnp.logical_not(last))
+                def _():
+                    left_sum(k + 1).wait_recv()
+                    add_in(1, k)
+
+            left_sum(k).start()
 
     def keep(j):
         return (j * 2 + px) * (1 - core) + (py * 2 + j) * core
@@ -546,14 +644,42 @@
         for side in range(2):
             parts[0, side, j, :, pl.ds(3 * width, width)] = value[side * rows : (side + 1) * rows]
 
-    pairs(fill_qkv)
+    filled = parts.shape[2]
+    for k in range(n_mp - 1, 0, -1):
+        pass_on(k)
+        if n_mp - 1 - k < filled:
+            fill_qkv(n_mp - 1 - k)
+    for j in range(n_mp - 1, filled):
+        fill_qkv(j)
     begin(0, 0)
 
-    for one in dx_copies:
-        one.wait()
-    dx = dxs[block(0), :].astype(F32)
-    for o in range(1, n_mp):
-        dx = dx + dxr[o - 1].astype(F32)
+    for k in range(1, n_mp):
+
+        @pl.when(me + k <= n_mp - 1)
+        def _(k=k):
+            right_sum(k).wait_send()
+
+        @pl.when(me >= k)
+        def _(k=k):
+            left_sum(k).wait_send()
+
+    @pl.when(first)
+    def _():
+        dxr[0, 0] = jnp.zeros_like(dxr[0, 0])
+
+    @pl.when(last)
+    def _():
+        dxr[1, 0] = jnp.zeros_like(dxr[1, 0])
+
+    @pl.when(jnp.logical_not(first))
+    def _():
+        right_sum(1).wait_recv()
+
+    @pl.when(jnp.logical_not(last))
+    def _():
+        left_sum(1).wait_recv()
+
+    dx = dxs[block(0), :].astype(F32) + dxr[0, 0].astype(F32) + dxr[1, 0].astype(F32)
     node = node_ref[...]
     inv = lax.rsqrt(jnp.mean(node * node, axis=-1, keepdims=True) + EPS)
     mean = jnp.mean(dx * node, axis=-1, keepdims=True)
@@ -571,13 +697,14 @@
     def edge_gather(i):
         at = span(i, TILE)
         place = lax.broadcasted_iota(jnp.int32, (TILE, 3 * nodes), 1)
-        table = (icol_ref[at, 1:2] == place).astype(F32) * aux_ref[at, attrs : attrs + 1]
+        aux = col_ref[at, :]
+        table = (aux[:, 1:2].astype(jnp.int32) == place).astype(F32) * aux[:, 2:3]
         msg_ref[at, :] = nn(table.astype(BF16), beside[...]).astype(BF16)
 
     loop(chunks, edge_gather)
 
     def fill_out(j):
-        value = tn(hid_ref[:, span(j, 2 * rows)], msg_ref[...]).astype(BF16)
+        value = nn(hid_t[span(j, 2 * rows), :], msg_ref[...]).astype(BF16)
         for side in range(2):
             parts[1, side, j] = value[side * rows : (side + 1) * rows]
 
@@ -589,13 +716,10 @@
 
     def edge_backward(i):
         at = span(i, TILE)
-        aux = aux_ref[at, :]
-        pre = pre_ref[at, :]
-        sigma = 1.0 / (1.0 + jnp.exp(-pre))
-        dpre = nt(msg_ref[at, :], w_out_ref[...])
-        dpre = dpre * sigma * (1.0 + pre * (1.0 - sigma)) * aux[:, attrs : attrs + 1]
+        aux = col_ref[at, :]
+        dpre = nt(msg_ref[at, :], w_out_ref[...]) * slope_ref[at, :]
         for a in range(attrs):
-            at_own[a : a + 1, :] += jnp.sum(aux[:, a : a + 1] * dpre, axis=0, keepdims=True)
+            at_own[a : a + 1, :] += jnp.sum(aux[:, 3 + a : 4 + a] * dpre, axis=0, keepdims=True)
         msg_ref[at, :] = dpre.astype(BF16)
 
     loop(chunks, edge_backward)
@@ -606,11 +730,11 @@
     ]
     attr_steps[0].start()
     place = lax.broadcasted_iota(jnp.int32, (grid_rows, edges), 0)
-    table = (irow_ref[0:1, :] == place).astype(F32).astype(BF16)
+    table = (source_ref[...] - me * grid_rows == place).astype(F32).astype(BF16)
     dproj_ref[...] = nn(table, msg_ref[...]).astype(BF16)
 
     def fill_in(j):
-        value = tn(grid_ref[:, span(j, 2 * rows)], dproj_ref[...]).astype(BF16)
+        value = nn(grid_t[span(j, 2 * rows), :], dproj_ref[...]).astype(BF16)
         for side in range(2):
             parts[2, side, j] = value[side * rows : (side + 1) * rows]
 
@@ -681,6 +805,18 @@
     collect(2, in_copies, d_in_ref)
 
 
+def write_out(*refs):
+    sems = refs[-1]
+    count = len(refs) // 2
+    copies = [
+        pltpu.make_async_copy(refs[i], refs[count + i], sems.at[i]) for i in range(count)
+    ]
+    for one in copies:
+        one.start()
+    for one in copies:
+        one.wait()
+
+
 def fused(
     grid_latent,
     mesh_latent,
@@ -696,7 +832,6 @@
     cotangent,
 ):
     n_dp, n_mp = lax.axis_size("dp"), lax.axis_size("mp")
-    band = lax.axis_index("mp")
     grid_rows, c = grid_latent.shape[1:]
     nodes = mesh_latent.shape[1]
     edges = edge_source.shape[1]
@@ -704,9 +839,6 @@
     width = w_qkv.shape[2]
     total = nodes * n_mp
     rows, cols = c // n_dp, c // n_mp
-    live = (jnp.arange(edges, dtype=jnp.int32) < edge_count[0, 0]).astype(F32)
-    irow = jnp.concatenate([edge_source - band * grid_rows, edge_dest - (band - 1) * nodes], axis=0)
-    aux = jnp.concatenate([edge_attr[0], live[None]], axis=0).T
     vmem = pl.BlockSpec(memory_space=pltpu.VMEM)
     shape = jax.ShapeDtypeStruct
     dma = pltpu.SemaphoreType.DMA
@@ -721,13 +853,17 @@
             shape((3, rows, width), F32),
             shape((width, rows), F32),
         ),
-        in_specs=[vmem] * 11,
+        in_specs=[vmem] * 12,
         out_specs=[vmem] * 7,
         scratch_shapes=[
             pltpu.VMEM((2 * grid_rows, c), BF16),
             pltpu.VMEM((edges, c), F32),
             pltpu.VMEM((edges, c), BF16),
+            pltpu.VMEM((c, edges), BF16),
+            pltpu.VMEM((c, grid_rows), BF16),
             pltpu.VMEM((edges, c), BF16),
+            pltpu.VMEM(((attrs + 10) // 8 * 8, edges), F32),
+            pltpu.VMEM((edges, (attrs + 10) // 8 * 8), F32),
             pltpu.VMEM((2, nodes, c), BF16),
             pltpu.VMEM((2, nodes, c), BF16),
             pltpu.VMEM((nodes, c), F32),
@@ -737,7 +873,7 @@
             pltpu.VMEM((3, total, width), BF16),
             pltpu.VMEM((total, width), BF16),
             pltpu.VMEM((total, c), BF16),
-            pltpu.VMEM((n_mp - 1, nodes, c), BF16),
+            pltpu.VMEM((2, n_mp - 1, nodes, c), BF16),
             pltpu.VMEM((3 * nodes, c), BF16),
             pltpu.VMEM((grid_rows, c), BF16),
             pltpu.VMEM((3, 2, n_dp // 2, rows, c), BF16),
@@ -749,10 +885,10 @@
             pltpu.VMEM((attrs, c), F32),
             pltpu.VMEM((3, attrs, c), F32),
             pltpu.VMEM((n_mp, attrs, c), F32),
-            dma((n_mp - 1, 2)),
-            dma((n_mp - 1, 2)),
+            dma((2, n_mp - 1, 2)),
+            dma((2, n_mp - 1, 2)),
             dma((2, 2)),
-            dma((n_mp - 1, 2)),
+            dma((2, n_mp - 1, 2)),
             dma((2, 2)),
             dma((3, 4, 2)),
             dma((2, n_mp - 1, 2)),
@@ -764,9 +900,10 @@
     )(
         grid_latent[0],
         mesh_latent[0],
-        irow.T,
-        irow,
-        aux,
+        edge_source,
+        edge_dest,
+        edge_count,
+        edge_attr[0],
         w_attr,
         w_in,
         w_out,
@@ -774,6 +911,14 @@
         w_o,
         cotangent[0],
     )
+    anywhere = pl.BlockSpec(memory_space=pl.ANY)
+    outs = pl.pallas_call(
+        write_out,
+        out_shape=tuple(shape(one.shape, one.dtype) for one in outs),
+        in_specs=[anywhere] * len(outs),
+        out_specs=[anywhere] * len(outs),
+        scratch_shapes=[dma((len(outs),))],
+    )(*outs)
     return (outs[0][None], outs[1][None]) + tuple(outs[2:])
 
 

time: 153 us -> 179 us (1.17)
  Pallas kernels: 138 us -> 178 us
  local copies, waits for them, and re-layouts: 11.3 us -> 0 us
  other arithmetic: 2.04 us -> 0 us
    pallas_call x0 -> x1, Pallas kernels: none -> 49.3 us  [fused(): pl.pallas_call(write_out, out_shape=tuple((shape(one.shape, one.dtype) fo...]
    unnamed x11 -> x0, local copies, waits for them, and re-layouts: 9.46 us -> none
    pallas_call x1, Pallas kernels: 138 us -> 128 us  [fused(): pl.pallas_call(functools.partial(layer_kernel, n_mp), out_shape=(shape((g...]
where the time goes in v2:
time: 179 us
  Pallas kernels  178 us (99%)
    pallas_call x1, Pallas kernels, fused(): pl.pallas_call(functools.partial(layer_kernel, n_mp), out_shape=(shape((g...  128 us
    pallas_call x1, Pallas kernels, fused(): pl.pallas_call(write_out, out_shape=tuple((shape(one.shape, one.dtype) fo...  49.3 us

profile of v2, /device:TPU:0, one launch (start us, length us, event | category | flops | bytes accessed | tf_op | source)
XLA Modules:
  0.0 179.2 jit_solution(7974515709048266885)
XLA Ops:
  1.3 128.4 %shard_map.171 = (bf16[256,1024]{1,0:T(8,128)(2,1)}, bf16[128,1024]{1,0:T(8,128)(2,1)}, f32[4,1024]{1,0:T(4,128)}, f32[128,256]{1,0:T(8,128)}, f32[128,256]{1,0:...) custom-call(bf16[256,1024]{1,0:T(8,128)(2,1)} %bitcast.6, bf16[128,1024]{1,0:T(8,128)(2,1)} %bitcast.7, ...), custom_call_target="tpu_custom_call" | custom-call | tf_op jit(solution)/shard_map/pallas_call | solution.py:845
  129.7 49.3 %shard_map.172 = (bf16[256,1024]{1,0:T(8,128)(2,1)}, bf16[128,1024]{1,0:T(8,128)(2,1)}, f32[4,1024]{1,0:T(4,128)}, f32[128,256]{1,0:T(8,128)}, f32[128,256]{1,0:...) custom-call(bf16[256,1024]{1,0:T(8,128)(2,1)} %get-tuple-element.21.refs_0_, ...), custom_call_target="tpu_custom_call" | custom-call | tf_op jit(solution)/shard_map/pallas_call | solution.py:915

commit v3 on v2

--- a/solution.py
+++ b/solution.py
@@ -250,9 +250,9 @@
     attr_ref,
     w_attr_ref,
     w_in_ref,
-    w_out_ref,
-    w_qkv_ref,
-    w_o_ref,
+    w_out_hbm,
+    w_qkv_hbm,
+    w_o_hbm,
     cot_ref,
     d_grid_ref,
     d_mesh_ref,
@@ -261,6 +261,9 @@
     d_out_ref,
     d_qkv_ref,
     d_o_ref,
+    w_out_ref,
+    w_qkv_ref,
+    w_o_ref,
     split_ref,
     slope_ref,
     hid_ref,
@@ -287,6 +290,7 @@
     r3,
     mpb,
     mpr,
+    dpre_ref,
     at_own,
     at_recv,
     at_all,
@@ -298,6 +302,7 @@
     rs_sem,
     mp_sem,
     at_sem,
+    w_sem,
 ):
     d = lax.axis_index("dp")
     me = lax.axis_index("mp")
@@ -320,7 +325,7 @@
     width = w_o_ref.shape[0]
     total = nodes * n_mp
     rows = parts.shape[3]
-    cols = mpb.shape[3]
+    cols = 2 * mpb.shape[3]
     scale = HDIM ** (-0.5)
     chunks = edges // TILE
 
@@ -333,6 +338,14 @@
             device_id=to,
             device_id_type=pl.DeviceIdType.MESH,
         )
+
+    loads = [
+        pltpu.make_async_copy(w_out_hbm, w_out_ref, w_sem.at[0]),
+        pltpu.make_async_copy(w_qkv_hbm, w_qkv_ref, w_sem.at[1]),
+        pltpu.make_async_copy(w_o_hbm, w_o_ref, w_sem.at[2]),
+    ]
+    for one in loads:
+        one.start()
 
     barrier = pltpu.get_barrier_semaphore()
     greeted = [by_core, by_x, by_y] + [along(o) for o in range(1, n_mp)]
@@ -439,12 +452,13 @@
         hid_ref[at, :] = hidden
         msg_ref[at, :] = nn(hidden, w_out_ref[...]).astype(BF16)
 
+    loads[0].wait()
+    hops = 1
     for i in range(chunks):
         edge_forward(i)
-        if i + 1 < n_mp:
-            cot_hop(i + 1)
-    for t in range(chunks + 1, n_mp):
-        cot_hop(t)
+        if hops < n_mp - 1:
+            cot_hop(hops)
+            hops = hops + 1
 
     dest = dest_ref[...] - (me - 1) * nodes
     place = lax.broadcasted_iota(jnp.int32, (2 * nodes, edges), 0)
@@ -483,6 +497,8 @@
             lower.wait_recv()
 
     exchange(down, up, hrecv.at[0], hrecv.at[1])
+    for t in range(hops, n_mp):
+        cot_hop(t)
     place = lax.broadcasted_iota(jnp.int32, (nodes, edges), 0) + nodes
     node = mesh_ref[...].astype(F32) + nn(
         (dest == place).astype(F32).astype(BF16), msg_ref[...]
@@ -501,8 +517,10 @@
         for i in range(3):
             qkvg[i, block(o), :] = nn(band, w_qkv_ref[i]).astype(BF16)
 
+    loads[1].wait()
     qkv(0)
     cot_drain()
+    loads[2].wait()
     qkvg[3] = nt(cot_all[...], w_o_ref[...]).astype(BF16)
 
     def turn(j):
@@ -630,28 +648,35 @@
             one.wait()
         return parts[group, core, py * 2 + px].astype(F32) + r3[group].astype(F32)
 
-    def pairs(fill):
+    def put(group, j, value, start=0):
+        value = value.astype(BF16)
+        for side in range(2):
+            parts[group, side, j, :, start : start + value.shape[1]] = value[
+                side * rows : (side + 1) * rows
+            ]
+
+    def pairs(group, fill):
         loop(parts.shape[2], fill)
-
-    def fill_qkv(j):
+        begin(group, 0)
+
+    def fill_qk(j):
+        x_part = x_all[:, span(j, 2 * rows)]
+        for i in range(2):
+            put(0, j, tn(x_part, dqkv[i]), i * width)
+
+    def fill_vo(j):
         at = span(j, 2 * rows)
-        x_part = x_all[:, at]
-        for i in range(3):
-            value = tn(x_part, dqkv[i]).astype(BF16)
-            for side in range(2):
-                parts[0, side, j, :, pl.ds(i * width, width)] = value[side * rows : (side + 1) * rows]
-        value = tn(cot_all[:, at], att_ref[...]).astype(BF16)
-        for side in range(2):
-            parts[0, side, j, :, pl.ds(3 * width, width)] = value[side * rows : (side + 1) * rows]
-
-    filled = parts.shape[2]
+        put(1, j, tn(x_all[:, at], dqkv[2]))
+        put(1, j, tn(cot_all[:, at], att_ref[...]), width)
+
+    fills = [functools.partial(pairs, 0, fill_qk), functools.partial(pairs, 1, fill_vo)]
     for k in range(n_mp - 1, 0, -1):
         pass_on(k)
-        if n_mp - 1 - k < filled:
-            fill_qkv(n_mp - 1 - k)
-    for j in range(n_mp - 1, filled):
-        fill_qkv(j)
-    begin(0, 0)
+        if fills:
+            fills.pop(0)()
+    for fill in fills:
+        fill()
+    finish_first(0)
 
     for k in range(1, n_mp):
 
@@ -691,7 +716,7 @@
     up = copy(middle, low, beside_sem.at[1], along(1))
     exchange(down, up, low, high)
     d_mesh_ref[...] = dnode.astype(BF16)
-    finish_first(0)
+    finish_first(1)
     settle(down, up)
 
     def edge_gather(i):
@@ -703,90 +728,110 @@
 
     loop(chunks, edge_gather)
 
-    def fill_out(j):
-        value = nn(hid_t[span(j, 2 * rows), :], msg_ref[...]).astype(BF16)
-        for side in range(2):
-            parts[1, side, j] = value[side * rows : (side + 1) * rows]
-
-    pairs(fill_out)
-    begin(1, 0)
+    half = cols // 2
+
+    def pieces(h):
+        return [pl.ds(t * cols + h * half, half) for t in range(n_mp)]
+
+    def columns(ref, at, h):
+        return jnp.concatenate([ref[at, piece] for piece in pieces(h)], axis=1)
+
+    def grad_out(h):
+        def fill(j):
+            put(2 + h, j, nn(hid_t[span(j, 2 * rows), :], columns(msg_ref, pl.ds(0, edges), h)))
+
+        pairs(2 + h, fill)
+
+    grad_out(0)
     finish_second(0)
+    grad_out(1)
+    finish_second(1)
+    finish_first(2)
 
     at_own[...] = jnp.zeros_like(at_own)
-
-    def edge_backward(i):
-        at = span(i, TILE)
-        aux = col_ref[at, :]
-        dpre = nt(msg_ref[at, :], w_out_ref[...]) * slope_ref[at, :]
-        for a in range(attrs):
-            at_own[a : a + 1, :] += jnp.sum(aux[:, 3 + a : 4 + a] * dpre, axis=0, keepdims=True)
-        msg_ref[at, :] = dpre.astype(BF16)
-
-    loop(chunks, edge_backward)
-    finish_first(1)
+    place = lax.broadcasted_iota(jnp.int32, (grid_rows, edges), 0)
+    source_table = (source_ref[...] - me * grid_rows == place).astype(F32).astype(BF16)
+
+    def grad_in(h):
+        def edge_backward(i):
+            at = span(i, TILE)
+            aux = col_ref[at, :]
+            weight = jnp.concatenate([w_out_ref[piece, :] for piece in pieces(h)], axis=0)
+            dpre = nt(msg_ref[at, :], weight) * columns(slope_ref, at, h)
+            for a in range(attrs):
+                value = jnp.sum(aux[:, 3 + a : 4 + a] * dpre, axis=0, keepdims=True)
+                for t, piece in enumerate(pieces(h)):
+                    at_own[a : a + 1, piece] += value[:, t * half : (t + 1) * half]
+            dpre_ref[at, :] = dpre.astype(BF16)
+
+        loop(chunks, edge_backward)
+        dproj = nn(source_table, dpre_ref[...]).astype(BF16)
+        for t, piece in enumerate(pieces(h)):
+            dproj_ref[:, piece] = dproj[:, t * half : (t + 1) * half]
+
+        def fill(j):
+            put(4 + h, j, nn(grid_t[span(j, 2 * rows), :], columns(dproj_ref, pl.ds(0, grid_rows), h)))
+
+        pairs(4 + h, fill)
+
+    grad_in(0)
+    finish_first(3)
+    finish_second(2)
+    grad_in(1)
+    finish_first(4)
+    finish_second(3)
 
     attr_steps = [
         copy(at_own, at_recv.at[i], at_sem.at[i], to) for i, to in enumerate((by_core, by_x, by_y))
     ]
     attr_steps[0].start()
-    place = lax.broadcasted_iota(jnp.int32, (grid_rows, edges), 0)
-    table = (source_ref[...] - me * grid_rows == place).astype(F32).astype(BF16)
-    dproj_ref[...] = nn(table, msg_ref[...]).astype(BF16)
-
-    def fill_in(j):
-        value = nn(grid_t[span(j, 2 * rows), :], dproj_ref[...]).astype(BF16)
-        for side in range(2):
-            parts[2, side, j] = value[side * rows : (side + 1) * rows]
-
-    pairs(fill_in)
-    begin(2, 0)
-    finish_second(1)
+
+    def grid_back(j):
+        at = span(j, 2 * TILE)
+        d_grid_ref[:, at] = nt(dproj_ref[...], w_in_ref[at, :]).astype(BF16)
+
+    finish_first(5)
+    loop(c // (2 * TILE), grid_back)
     attr_steps[0].wait()
     at_own[...] = at_own[...] + at_recv[0]
     attr_steps[1].start()
-
-    def grid_back(j):
-        at = span(j, 2 * TILE)
-        d_grid_ref[:, at] = nt(dproj_ref[...], w_in_ref[at, :]).astype(BF16)
-
-    finish_first(2)
-    loop(c // (2 * TILE), grid_back)
-
     value = finish_third(0)
-    for i in range(3):
+    for i in range(2):
         d_qkv_ref[i] = value[:, i * width : (i + 1) * width]
-    d_o_ref[...] = value[:, 3 * width :].T
-    attr_steps[1].wait()
-    at_own[...] = at_own[...] + at_recv[1]
-    attr_steps[2].start()
+    value = finish_third(1)
+    d_qkv_ref[2] = value[:, :width]
+    d_o_ref[...] = value[:, width:].T
 
     def spread(group):
+        slot = group - 2
         value = finish_third(group)
         for t in range(n_mp):
-            mpb[group - 1, t] = value[:, t * cols : (t + 1) * cols].astype(BF16)
+            mpb[slot, t] = value[:, t * half : (t + 1) * half].astype(BF16)
         copies = [
-            copy(
-                mpb.at[group - 1, (me + o) % n_mp],
-                mpr.at[group - 1, o - 1],
-                mp_sem.at[group - 1, o - 1],
-                along(o),
-            )
+            copy(mpb.at[slot, (me + o) % n_mp], mpr.at[slot, o - 1], mp_sem.at[slot, o - 1], along(o))
             for o in range(1, n_mp)
         ]
         for one in copies:
             one.start()
         return copies
 
-    def collect(group, copies, out_ref):
+    def collect(group, copies, out_ref, h):
+        slot = group - 2
         for one in copies:
             one.wait()
-        value = mpb[group - 1, me].astype(F32)
+        value = mpb[slot, me].astype(F32)
         for o in range(1, n_mp):
-            value = value + mpr[group - 1, o - 1].astype(F32)
-        out_ref[...] = value
-
-    out_copies = spread(1)
-    finish_second(2)
+            value = value + mpr[slot, o - 1].astype(F32)
+        out_ref[:, h * half : (h + 1) * half] = value
+
+    copies = [spread(2)]
+    finish_second(4)
+    copies.append(spread(3))
+    attr_steps[1].wait()
+    at_own[...] = at_own[...] + at_recv[1]
+    attr_steps[2].start()
+    finish_second(5)
+    copies.append(spread(4))
     attr_steps[2].wait()
     at_all[0] = at_own[...] + at_recv[2]
     attr_copies = [
@@ -794,15 +839,17 @@
     ]
     for one in attr_copies:
         one.start()
-    in_copies = spread(2)
+    copies.append(spread(5))
+    collect(2, copies[0], d_out_ref, 0)
+    collect(3, copies[1], d_out_ref, 1)
     for one in attr_copies:
         one.wait()
     value = at_all[me]
     for s in range(1, n_mp):
         value = value + at_all[(me + n_mp - s) % n_mp]
     d_attr_ref[...] = value
-    collect(1, out_copies, d_out_ref)
-    collect(2, in_copies, d_in_ref)
+    collect(4, copies[2], d_in_ref, 0)
+    collect(5, copies[3], d_in_ref, 1)
 
 
 def write_out(*refs):
@@ -840,6 +887,7 @@
     total = nodes * n_mp
     rows, cols = c // n_dp, c // n_mp
     vmem = pl.BlockSpec(memory_space=pltpu.VMEM)
+    anywhere = pl.BlockSpec(memory_space=pl.ANY)
     shape = jax.ShapeDtypeStruct
     dma = pltpu.SemaphoreType.DMA
     outs = pl.pallas_call(
@@ -853,9 +901,12 @@
             shape((3, rows, width), F32),
             shape((width, rows), F32),
         ),
-        in_specs=[vmem] * 12,
+        in_specs=[vmem] * 8 + [anywhere] * 3 + [vmem],
         out_specs=[vmem] * 7,
         scratch_shapes=[
+            pltpu.VMEM(w_out.shape, BF16),
+            pltpu.VMEM(w_qkv.shape, BF16),
+            pltpu.VMEM(w_o.shape, BF16),
             pltpu.VMEM((2 * grid_rows, c), BF16),
             pltpu.VMEM((edges, c), F32),
             pltpu.VMEM((edges, c), BF16),
@@ -876,12 +927,13 @@
             pltpu.VMEM((2, n_mp - 1, nodes, c), BF16),
             pltpu.VMEM((3 * nodes, c), BF16),
             pltpu.VMEM((grid_rows, c), BF16),
-            pltpu.VMEM((3, 2, n_dp // 2, rows, c), BF16),
-            pltpu.VMEM((3, n_dp // 2, rows, c), BF16),
-            pltpu.VMEM((3, 2, rows, c), BF16),
-            pltpu.VMEM((3, rows, c), BF16),
-            pltpu.VMEM((2, n_mp, rows, cols), BF16),
-            pltpu.VMEM((2, n_mp - 1, rows, cols), BF16),
+            pltpu.VMEM((6, 2, n_dp // 2, rows, c // 2), BF16),
+            pltpu.VMEM((6, n_dp // 2, rows, c // 2), BF16),
+            pltpu.VMEM((6, 2, rows, c // 2), BF16),
+            pltpu.VMEM((6, rows, c // 2), BF16),
+            pltpu.VMEM((4, n_mp, rows, cols // 2), BF16),
+            pltpu.VMEM((4, n_mp - 1, rows, cols // 2), BF16),
+            pltpu.VMEM((edges, c // 2), BF16),
             pltpu.VMEM((attrs, c), F32),
             pltpu.VMEM((3, attrs, c), F32),
             pltpu.VMEM((n_mp, attrs, c), F32),
@@ -890,9 +942,10 @@
             dma((2, 2)),
             dma((2, n_mp - 1, 2)),
             dma((2, 2)),
-            dma((3, 4, 2)),
-            dma((2, n_mp - 1, 2)),
+            dma((6, 4, 2)),
+            dma((4, n_mp - 1, 2)),
             dma((2 + n_mp, 2)),
+            dma((3,)),
         ],
         compiler_params=pltpu.CompilerParams(
             collective_id=0, has_side_effects=True, vmem_limit_bytes=58 * 2**20
@@ -911,11 +964,10 @@
         w_o,
         cotangent[0],
     )
-    anywhere = pl.BlockSpec(memory_space=pl.ANY)
     outs = pl.pallas_call(
         write_out,
         out_shape=tuple(shape(one.shape, one.dtype) for one in outs),
-        in_specs=[anywhere] * len(outs),
+        in_specs=[vmem] * len(outs),
         out_specs=[anywhere] * len(outs),
         scratch_shapes=[dma((len(outs),))],
     )(*outs)
@@ -931,7 +983,7 @@
         and n_mp % 2 == 0
         and n_mp * mesh_latent.shape[1] <= 512
         and 4 * width == c
-        and width % LANES == 0
+        and width % (2 * LANES) == 0
         and c % (2 * TILE) == 0
         and (c // n_dp) % LANES == 0
         and edge_source.shape[1] % TILE == 0

time: 179 us -> 124 us (0.69)
  Pallas kernels: 178 us -> 122 us
    pallas_call x1, Pallas kernels: 49.3 us -> 2.58 us  [fused(): pl.pallas_call(write_out, out_shape=tuple((shape(one.shape, one.dtype) fo...]
    pallas_call x1, Pallas kernels: 128 us -> 120 us  [fused(): pl.pallas_call(functools.partial(layer_kernel, n_mp), out_shape=(shape((g...]
where the time goes in v3:
time: 124 us
  Pallas kernels  122 us (98%)
  between operations  1.45 us (1%)
    pallas_call x1, Pallas kernels, fused(): pl.pallas_call(functools.partial(layer_kernel, n_mp), out_shape=(shape((g...  120 us
    pallas_call x1, Pallas kernels, fused(): pl.pallas_call(write_out, out_shape=tuple((shape(one.shape, one.dtype) fo...  2.58 us

profile of v3, /device:TPU:0, one launch (start us, length us, event | category | flops | bytes accessed | tf_op | source)
XLA Modules:
  0.0 123.6 jit_solution(8496437475927911356)
XLA Ops:
  1.3 119.6 %shard_map.171 = (bf16[256,1024]{1,0:T(8,128)(2,1)}, bf16[128,1024]{1,0:T(8,128)(2,1)}, f32[4,1024]{1,0:T(4,128)}, f32[128,256]{1,0:T(8,128)}, f32[128,256]{1,0:...) custom-call(bf16[256,1024]{1,0:T(8,128)(2,1)} %bitcast.6, bf16[128,1024]{1,0:T(8,128)(2,1)} %bitcast.7, ...), custom_call_target="tpu_custom_call" | custom-call | tf_op jit(solution)/shard_map/pallas_call | solution.py:893
  120.9 2.6 %shard_map.172 = (bf16[256,1024]{1,0:T(8,128)(2,1)}, bf16[128,1024]{1,0:T(8,128)(2,1)}, f32[4,1024]{1,0:T(4,128)}, f32[128,256]{1,0:T(8,128)}, f32[128,256]{1,0:...) custom-call(bf16[256,1024]{1,0:T(8,128)(2,1)} %get-tuple-element.21.refs_0_, ...), custom_call_target="tpu_custom_call" | custom-call | tf_op jit(solution)/shard_map/pallas_call | solution.py:967

commit v4 on v3

--- a/solution.py
+++ b/solution.py
@@ -291,6 +291,10 @@
     mpb,
     mpr,
     dpre_ref,
+    table_ref,
+    dest_table_ref,
+    gather_ref,
+    source_table,
     at_own,
     at_recv,
     at_all,
@@ -327,7 +331,6 @@
     rows = parts.shape[3]
     cols = 2 * mpb.shape[3]
     scale = HDIM ** (-0.5)
-    chunks = edges // TILE
 
     def copy(src, dst, sems, to):
         return pltpu.make_async_remote_copy(
@@ -436,38 +439,52 @@
 
     loop(c // (2 * TILE), project)
 
-    def edge_forward(i):
-        at = span(i, TILE)
-        aux = col_ref[at, :]
-        place = lax.broadcasted_iota(jnp.int32, (TILE, grid_rows), 1)
-        table = (aux[:, 0:1].astype(jnp.int32) == place).astype(F32).astype(BF16)
-        table = jnp.concatenate([table, table], axis=1)
-        pre = nn(table, split_ref[...])
+    source = col_ref[:, 0:1].astype(jnp.int32)
+    place = lax.broadcasted_iota(jnp.int32, (edges, grid_rows), 1)
+    table = (source == place).astype(F32).astype(BF16)
+    table_ref[:, pl.ds(0, grid_rows)] = table
+    table_ref[:, pl.ds(grid_rows, grid_rows)] = table
+
+    def activate(j):
+        at = span(j, TILE)
+        pre = nn(table_ref[...], split_ref[:, at])
         for a in range(attrs):
-            pre = pre + aux[:, 3 + a : 4 + a] * w_attr_ref[a : a + 1, :]
+            pre = pre + col_ref[:, 3 + a : 4 + a] * w_attr_ref[a : a + 1, at]
         sigma = 1.0 / (1.0 + jnp.exp(-pre))
-        live = aux[:, 2:3]
-        slope_ref[at, :] = sigma * (1.0 + pre * (1.0 - sigma)) * live
-        hidden = (pre * sigma * live).astype(BF16)
-        hid_ref[at, :] = hidden
-        msg_ref[at, :] = nn(hidden, w_out_ref[...]).astype(BF16)
-
+        live = col_ref[:, 2:3]
+        slope_ref[:, at] = sigma * (1.0 + pre * (1.0 - sigma)) * live
+        hid_ref[:, at] = (pre * sigma * live).astype(BF16)
+
+    loop(c // TILE, activate)
+    cot_hop(1)
     loads[0].wait()
-    hops = 1
-    for i in range(chunks):
-        edge_forward(i)
-        if hops < n_mp - 1:
-            cot_hop(hops)
-            hops = hops + 1
+
+    def talk(j):
+        at = span(j, TILE)
+        msg_ref[:, at] = nn(hid_ref[...], w_out_ref[:, at]).astype(BF16)
+
+    loop(c // TILE, talk)
+    hops = min(2, n_mp - 1)
+    if hops < n_mp - 1:
+        cot_hop(hops)
+        hops = hops + 1
 
     dest = dest_ref[...] - (me - 1) * nodes
-    place = lax.broadcasted_iota(jnp.int32, (2 * nodes, edges), 0)
-    place = jnp.where(place < nodes, place, place + nodes)
-    sides = nn((dest == place).astype(F32).astype(BF16), msg_ref[...])
-    hsend[0] = sides[:nodes].astype(BF16)
-    hsend[1] = sides[nodes:].astype(BF16)
+    place = lax.broadcasted_iota(jnp.int32, (3 * nodes, edges), 0)
+    dest_table = (dest == place).astype(F32).astype(BF16)
+
+    def scatter(j):
+        at = span(j, TILE)
+        value = nn(dest_table_ref[...], msg_ref[:, at])
+        hsend[0, :, at] = value[:nodes].astype(BF16)
+        node_ref[:, at] = mesh_ref[:, at].astype(F32) + value[nodes : 2 * nodes]
+        hsend[1, :, at] = value[2 * nodes :].astype(BF16)
+
+    dest_table_ref[...] = dest_table
+    loop(c // TILE, scatter)
     down = copy(hsend.at[0], hrecv.at[1], halo_sem.at[0], along(-1))
     up = copy(hsend.at[1], hrecv.at[0], halo_sem.at[1], along(1))
+
     def exchange(lower, upper, low_slot, high_slot):
         @pl.when(jnp.logical_not(first))
         def _():
@@ -499,12 +516,8 @@
     exchange(down, up, hrecv.at[0], hrecv.at[1])
     for t in range(hops, n_mp):
         cot_hop(t)
-    place = lax.broadcasted_iota(jnp.int32, (nodes, edges), 0) + nodes
-    node = mesh_ref[...].astype(F32) + nn(
-        (dest == place).astype(F32).astype(BF16), msg_ref[...]
-    )
     settle(down, up)
-    node = node + hrecv[0].astype(F32) + hrecv[1].astype(F32)
+    node = node_ref[...] + hrecv[0].astype(F32) + hrecv[1].astype(F32)
     inv = lax.rsqrt(jnp.mean(node * node, axis=-1, keepdims=True) + EPS)
     node_ref[...] = node
     x_all[block(0), :] = (node * inv).astype(BF16)
@@ -529,6 +542,11 @@
         grid_t[at, :] = grid_ref[:, at].T
 
     loop(c // TILE, turn)
+    place = lax.broadcasted_iota(jnp.int32, (edges, 3 * nodes), 1)
+    table = (col_ref[:, 1:2].astype(jnp.int32) == place).astype(F32) * col_ref[:, 2:3]
+    gather_ref[...] = table.astype(BF16)
+    place = lax.broadcasted_iota(jnp.int32, (grid_rows, edges), 0)
+    source_table[...] = (source_ref[...] - me * grid_rows == place).astype(F32).astype(BF16)
     for t in range(1, n_mp):
         x_hop(t, qkv)
     x_drain()
@@ -719,28 +737,31 @@
     finish_first(1)
     settle(down, up)
 
-    def edge_gather(i):
-        at = span(i, TILE)
-        place = lax.broadcasted_iota(jnp.int32, (TILE, 3 * nodes), 1)
-        aux = col_ref[at, :]
-        table = (aux[:, 1:2].astype(jnp.int32) == place).astype(F32) * aux[:, 2:3]
-        msg_ref[at, :] = nn(table.astype(BF16), beside[...]).astype(BF16)
-
-    loop(chunks, edge_gather)
+    def edge_gather(j):
+        at = span(j, TILE)
+        msg_ref[:, at] = nn(gather_ref[...], beside[:, at]).astype(BF16)
+
+    loop(c // TILE, edge_gather)
 
     half = cols // 2
 
     def pieces(h):
         return [pl.ds(t * cols + h * half, half) for t in range(n_mp)]
 
-    def columns(ref, at, h):
-        return jnp.concatenate([ref[at, piece] for piece in pieces(h)], axis=1)
+    def spill(group, left, right_of):
+        for u in range(0, n_mp, 2):
+            value = nn(left[...], right_of(u)).astype(BF16)
+            for r in range(2 * parts.shape[2]):
+                parts[group, r % 2, r // 2, :, u * half : (u + 2) * half] = value[
+                    r * rows : (r + 1) * rows
+                ]
+        begin(group, 0)
+
+    def pair_of(ref, at, h, u):
+        return jnp.concatenate([ref[at, piece] for piece in pieces(h)[u : u + 2]], axis=1)
 
     def grad_out(h):
-        def fill(j):
-            put(2 + h, j, nn(hid_t[span(j, 2 * rows), :], columns(msg_ref, pl.ds(0, edges), h)))
-
-        pairs(2 + h, fill)
+        spill(2 + h, hid_t, lambda u: pair_of(msg_ref, pl.ds(0, edges), h, u))
 
     grad_out(0)
     finish_second(0)
@@ -748,31 +769,20 @@
     finish_second(1)
     finish_first(2)
 
-    at_own[...] = jnp.zeros_like(at_own)
-    place = lax.broadcasted_iota(jnp.int32, (grid_rows, edges), 0)
-    source_table = (source_ref[...] - me * grid_rows == place).astype(F32).astype(BF16)
-
     def grad_in(h):
-        def edge_backward(i):
-            at = span(i, TILE)
-            aux = col_ref[at, :]
-            weight = jnp.concatenate([w_out_ref[piece, :] for piece in pieces(h)], axis=0)
-            dpre = nt(msg_ref[at, :], weight) * columns(slope_ref, at, h)
+        for u in range(0, n_mp, 2):
+            spots = pieces(h)[u : u + 2]
+            weight = jnp.concatenate([w_out_ref[piece, :] for piece in spots], axis=0)
+            dpre = nt(msg_ref[...], weight) * pair_of(slope_ref, pl.ds(0, edges), h, u)
             for a in range(attrs):
-                value = jnp.sum(aux[:, 3 + a : 4 + a] * dpre, axis=0, keepdims=True)
-                for t, piece in enumerate(pieces(h)):
-                    at_own[a : a + 1, piece] += value[:, t * half : (t + 1) * half]
-            dpre_ref[at, :] = dpre.astype(BF16)
-
-        loop(chunks, edge_backward)
-        dproj = nn(source_table, dpre_ref[...]).astype(BF16)
+                value = jnp.sum(col_ref[:, 3 + a : 4 + a] * dpre, axis=0, keepdims=True)
+                for t, piece in enumerate(spots):
+                    at_own[a : a + 1, piece] = value[:, t * half : (t + 1) * half]
+            dpre_ref[:, u * half : (u + 2) * half] = dpre.astype(BF16)
+        dproj = nn(source_table[...], dpre_ref[...]).astype(BF16)
         for t, piece in enumerate(pieces(h)):
             dproj_ref[:, piece] = dproj[:, t * half : (t + 1) * half]
-
-        def fill(j):
-            put(4 + h, j, nn(grid_t[span(j, 2 * rows), :], columns(dproj_ref, pl.ds(0, grid_rows), h)))
-
-        pairs(4 + h, fill)
+        spill(4 + h, grid_t, lambda u: pair_of(dproj_ref, pl.ds(0, grid_rows), h, u))
 
     grad_in(0)
     finish_first(3)
@@ -934,6 +944,10 @@
             pltpu.VMEM((4, n_mp, rows, cols // 2), BF16),
             pltpu.VMEM((4, n_mp - 1, rows, cols // 2), BF16),
             pltpu.VMEM((edges, c // 2), BF16),
+            pltpu.VMEM((edges, 2 * grid_rows), BF16),
+            pltpu.VMEM((3 * nodes, edges), BF16),
+            pltpu.VMEM((edges, 3 * nodes), BF16),
+            pltpu.VMEM((grid_rows, edges), BF16),
             pltpu.VMEM((attrs, c), F32),
             pltpu.VMEM((3, attrs, c), F32),
             pltpu.VMEM((n_mp, attrs, c), F32),

time: 124 us -> 123 us (level)
    pallas_call x1, Pallas kernels: 120 us -> 118 us  [fused(): pl.pallas_call(functools.partial(layer_kernel, n_mp), out_shape=(shape((g...]
where the time goes in v4:
time: 123 us; the launch traced here: 122 us
  Pallas kernels  121 us (98%)
  between operations  1.45 us (1%)
    pallas_call x1, Pallas kernels, fused(): pl.pallas_call(functools.partial(layer_kernel, n_mp), out_shape=(shape((g...  118 us
    pallas_call x1, Pallas kernels, fused(): pl.pallas_call(write_out, out_shape=tuple((shape(one.shape, one.dtype) fo...  2.58 us

profile of v4, /device:TPU:0, one launch (start us, length us, event | category | flops | bytes accessed | tf_op | source)
XLA Modules:
  0.0 122.3 jit_solution(3796792178436034558)
XLA Ops:
  1.3 118.3 %shard_map.171 = (bf16[256,1024]{1,0:T(8,128)(2,1)}, bf16[128,1024]{1,0:T(8,128)(2,1)}, f32[4,1024]{1,0:T(4,128)}, f32[128,256]{1,0:T(8,128)}, f32[128,256]{1,0:...) custom-call(bf16[256,1024]{1,0:T(8,128)(2,1)} %bitcast.6, bf16[128,1024]{1,0:T(8,128)(2,1)} %bitcast.7, ...), custom_call_target="tpu_custom_call" | custom-call | tf_op jit(solution)/shard_map/pallas_call | solution.py:903
  119.6 2.6 %shard_map.172 = (bf16[256,1024]{1,0:T(8,128)(2,1)}, bf16[128,1024]{1,0:T(8,128)(2,1)}, f32[4,1024]{1,0:T(4,128)}, f32[128,256]{1,0:T(8,128)}, f32[128,256]{1,0:...) custom-call(bf16[256,1024]{1,0:T(8,128)(2,1)} %get-tuple-element.21.refs_0_, ...), custom_call_target="tpu_custom_call" | custom-call | tf_op jit(solution)/shard_map/pallas_call | solution.py:981

commit v5 on v4

--- a/solution.py
+++ b/solution.py
@@ -464,10 +464,6 @@
         msg_ref[:, at] = nn(hid_ref[...], w_out_ref[:, at]).astype(BF16)
 
     loop(c // TILE, talk)
-    hops = min(2, n_mp - 1)
-    if hops < n_mp - 1:
-        cot_hop(hops)
-        hops = hops + 1
 
     dest = dest_ref[...] - (me - 1) * nodes
     place = lax.broadcasted_iota(jnp.int32, (3 * nodes, edges), 0)
@@ -514,7 +510,7 @@
             lower.wait_recv()
 
     exchange(down, up, hrecv.at[0], hrecv.at[1])
-    for t in range(hops, n_mp):
+    for t in range(2, n_mp - 1):
         cot_hop(t)
     settle(down, up)
     node = node_ref[...] + hrecv[0].astype(F32) + hrecv[1].astype(F32)
@@ -532,6 +528,8 @@
 
     loads[1].wait()
     qkv(0)
+    if n_mp > 2:
+        cot_hop(n_mp - 1)
     cot_drain()
     loads[2].wait()
     qkvg[3] = nt(cot_all[...], w_o_ref[...]).astype(BF16)

time: 123 us -> 123 us (level)
  no operation moved by 1% of the time
where the time goes in v5:
time: 123 us
  Pallas kernels  122 us (99%)
  between operations  1.45 us (1%)
    pallas_call x1, Pallas kernels, fused(): pl.pallas_call(functools.partial(layer_kernel, n_mp), out_shape=(shape((g...  119 us
    pallas_call x1, Pallas kernels, fused(): pl.pallas_call(write_out, out_shape=tuple((shape(one.shape, one.dtype) fo...  2.58 us

profile of v5, /device:TPU:0, one launch (start us, length us, event | category | flops | bytes accessed | tf_op | source)
XLA Modules:
  0.0 123.3 jit_solution(13822543057545335327)
XLA Ops:
  1.3 119.3 %shard_map.171 = (bf16[256,1024]{1,0:T(8,128)(2,1)}, bf16[128,1024]{1,0:T(8,128)(2,1)}, f32[4,1024]{1,0:T(4,128)}, f32[128,256]{1,0:T(8,128)}, f32[128,256]{1,0:...) custom-call(bf16[256,1024]{1,0:T(8,128)(2,1)} %bitcast.6, bf16[128,1024]{1,0:T(8,128)(2,1)} %bitcast.7, ...), custom_call_target="tpu_custom_call" | custom-call | tf_op jit(solution)/shard_map/pallas_call | solution.py:901
  120.5 2.6 %shard_map.172 = (bf16[256,1024]{1,0:T(8,128)(2,1)}, bf16[128,1024]{1,0:T(8,128)(2,1)}, f32[4,1024]{1,0:T(4,128)}, f32[128,256]{1,0:T(8,128)}, f32[128,256]{1,0:...) custom-call(bf16[256,1024]{1,0:T(8,128)(2,1)} %get-tuple-element.21.refs_0_, ...), custom_call_target="tpu_custom_call" | custom-call | tf_op jit(solution)/shard_map/pallas_call | solution.py:979
